TPU v7x, 32 devices: a whole 2x2x4 slice. The times are simulated.
32 devices in a mesh: groups: 2 (over x), tile: 16 (over z, y, core).
Axes of the slice: x: 2, y: 2, z: 4, core: 2. Of those that a mesh axis runs over, the one named last changes fastest.
Arguments:
- probes: float32 [8, 262144], P(None, ('groups', 'tile')), parts along dimension 1, may hold values from -6 to 6
- level_set: float32 [262144], P(('groups', 'tile')), parts along dimension 0, may hold values from -6 to 6
- unit_label: int32 [262144], P(('groups', 'tile')), parts along dimension 0, may hold values from 0 to 3
- contrast: float32 [8], P('groups'), parts along dimension 0, may hold values from 0.2 to 1.5
- station_weight: float32 [65536], P('groups'), parts along dimension 0, may hold values from 0.2 to 2
- u_factor: bfloat16 [4096, 32, 512], P(('groups', 'tile')), parts along dimension 0, may hold values from -1 to 1
- v_factor: bfloat16 [4096, 32, 512], P(('groups', 'tile')), parts along dimension 0, may hold values from -0.25 to 0.25
- col_owner: int32 [4096, 1], P('groups'), parts along dimension 0, may hold values from 0 to 15; in each aligned block of 128 rows (0 to 127, 128 to 255, ...) at most 16 rows name the same one
- col_local: int32 [4096], P('groups'), parts along dimension 0, may hold values from 0 to 15
- row_owner: int32 [4096, 1], P('groups'), parts along dimension 0, may hold values from 0 to 15; in each aligned block of 128 rows (0 to 127, 128 to 255, ...) at most 16 rows name the same one
- row_local: int32 [4096], P('groups'), parts along dimension 0, may hold values from 0 to 3
- tile_rank: int32 [4096], P('groups'), parts along dimension 0, may hold values from 8 to 32
Outputs:
- hessian_probes: float32 [8, 262144], P(None, ('groups', 'tile')), parts along dimension 1
There are 2 independent parts, one for each index of `groups`. A program takes and returns all parts, laid end to end along the dimension named above; each array names one. Nothing has to cross between parts.
Inputs may be any that keep to these rules, and one draw needn't show every extreme that they name: `col_owner`: among the 128 tiles of one device (aligned blocks of 128 entries) no owner is named more than 16 times, a bound that some block reaches. `row_owner`: among the 128 tiles of one device (aligned blocks of 128 entries) no owner is named more than 16 times, a bound that some block reaches.
All inputs are finite; a program needn't handle non-finite values.
Results may differ from a plain program's by a relative error of at most 0.005.
Values may be sent and summed in bfloat16 or wider, within the bound.
A program may use at most 64 MiB of HBM per device.

v0:
```python
import functools

import jax
import jax.numpy as jnp
from jax import lax
from jax.experimental import pallas as pl
from jax.experimental.pallas import tpu as pltpu
from jax.sharding import PartitionSpec as P

MESH = pl.DeviceIdType.MESH
VMEM_LIMIT = 56 * 1024 * 1024
GROUP = 8
F32 = jnp.float32
BF16 = jnp.bfloat16


def place(lines):
    me = lax.axis_index("tile")
    core = lax.rem(me, 2)
    side = lax.rem(me // 2, 2)
    step = me // 4
    return me, core, side, step


def index_of(step, side, core):
    return (step * 2 + side) * 2 + core


def enter(lines, step, side, core):
    barrier = pltpu.get_barrier_semaphore()
    for d in range(1, lines):
        peer = index_of(lax.rem(step + d, lines), side, core)
        pl.semaphore_signal(barrier, inc=1, device_id={"tile": peer}, device_id_type=MESH)
    for peer in (index_of(step, 1 - side, core), index_of(step, side, 1 - core)):
        pl.semaphore_signal(barrier, inc=1, device_id={"tile": peer}, device_id_type=MESH)
    pl.semaphore_wait(barrier, lines + 1)


def remote(src, dst, send, recv, peer):
    return pltpu.make_async_remote_copy(
        src_ref=src,
        dst_ref=dst,
        send_sem=send,
        recv_sem=recv,
        device_id={"tile": peer},
        device_id_type=MESH,
    )


def gather_shards(lines, own, out, local_sem, sems, step, side, core):
    send_z, recv_z, send_y, recv_y, send_c, recv_c = sems
    me = index_of(step, side, core)
    across = index_of(step, 1 - side, core)
    twin = index_of(step, side, 1 - core)
    started = []

    def go(src, slot, send, recv, peer):
        copy = remote(src, out.at[slot], send, recv, peer)
        copy.start()
        started.append(copy)

    go(own, me, send_y.at[0], recv_y.at[0], across)
    for d in range(1, lines):
        peer = index_of(lax.rem(step + d, lines), side, core)
        go(own, me, send_z.at[d - 1], recv_z.at[d - 1], peer)
    go(own, me, send_c.at[0], recv_c.at[0], twin)
    mine = pltpu.make_async_copy(own, out.at[me], local_sem)
    mine.start()

    def arrived(slot, recv, peer):
        remote(out.at[slot], out.at[slot], recv, recv, peer).wait_recv()

    for k in range(lines + 1):
        if 1 <= k < lines:
            slot = index_of(lax.rem(step + lines - k, lines), side, core)
            arrived(slot, recv_z.at[k - 1], me)
            go(out.at[slot], slot, send_y.at[k], recv_y.at[k], across)
            go(out.at[slot], slot, send_c.at[k], recv_c.at[k], twin)
        if k >= 1:
            j = k - 1
            slot = index_of(lax.rem(step + lines - j, lines), 1 - side, core)
            arrived(slot, recv_y.at[j], across)
            go(out.at[slot], slot, send_c.at[lines + j], recv_c.at[lines + j], twin)
    for k in range(lines):
        for far in range(2):
            where = 1 - side if far else side
            slot = index_of(lax.rem(step + lines - k, lines), where, 1 - core)
            arrived(slot, recv_c.at[far * lines + k], twin)
    mine.wait()
    for copy in started:
        copy.wait_send()


def gather_sems(lines):
    dma = pltpu.SemaphoreType.DMA
    return [
        dma((lines - 1,)),
        dma((lines - 1,)),
        dma((lines,)),
        dma((lines,)),
        dma((2 * lines,)),
        dma((2 * lines,)),
    ]


def cell_scaling(level, label, contrast, units):
    picked = jnp.full(level.shape, contrast[0], F32)
    for unit in range(1, units):
        picked = jnp.where(label == unit, contrast[unit], picked)
    return picked / (1.0 + level * level)


def halves(block):
    half = block.shape[1] // 2
    return jnp.concatenate([block[:, :half], block[:, half:]], axis=0)


def cells_kernel(lines, units, contrast, probes, level, label, out, own, local_sem, *sems):
    _, core, side, step = place(lines)
    enter(lines, step, side, core)
    count = own.shape[0]
    width = probes.shape[1] // count
    for b in range(count):
        cut = pl.ds(b * width, width)
        scaling = cell_scaling(level[:, cut], label[:, cut], contrast, units)
        own[b] = halves(probes[:, cut] * scaling).astype(BF16)
    gather_shards(lines, own, out, local_sem, sems, step, side, core)


def tiles_kernel(
    per_step, rank_max, take, put, ranks, held, first, second, out, total
):
    i = pl.program_id(0)

    @pl.when(i == 0)
    def _():
        total[...] = jnp.zeros_like(total)

    rows = GROUP * rank_max
    lane = lax.broadcasted_iota(jnp.int32, (8, rows), 1)
    groups = range(per_step // GROUP)
    inners = []
    for g in groups:
        pieces = []
        for j in range(GROUP):
            block = held[take[i * per_step + g * GROUP + j]].astype(F32)
            pieces.append(jnp.concatenate([block[:8], block[8:]], axis=1))
        data = jnp.concatenate(pieces, axis=0).astype(BF16)
        inners.append(
            lax.dot_general(
                data,
                first[g * rows : (g + 1) * rows],
                (((1,), (1,)), ((), ())),
                preferred_element_type=F32,
            )
        )
    results = []
    for g in groups:
        kept = []
        for j in range(GROUP):
            start = j * rank_max
            end = start + ranks[i * per_step + g * GROUP + j]
            part = inners[g][j * 8 : (j + 1) * 8]
            kept.append(jnp.where((lane >= start) & (lane < end), part, 0.0))
        coeff = jnp.concatenate(kept, axis=0).astype(BF16)
        results.append(
            jnp.dot(coeff, second[g * rows : (g + 1) * rows], preferred_element_type=F32)
        )
    for g in groups:
        for j in range(GROUP):
            spot = put[i * per_step + g * GROUP + j]
            total[spot] += results[g][j * 8 : (j + 1) * 8]

    @pl.when(i == pl.num_programs(0) - 1)
    def _():
        out[...] = total[...].reshape(out.shape).astype(out.dtype)


def apply_tiles(take, put, ranks, held, first, second, blocks, dtype, rank_max):
    tiles = take.shape[0]
    per_step = 4 * GROUP
    width = second.shape[1]
    rows = per_step * rank_max
    spec = pl.BlockSpec((rows, width), lambda i, *_: (i, 0))
    return pl.pallas_call(
        functools.partial(tiles_kernel, per_step, rank_max),
        out_shape=jax.ShapeDtypeStruct((blocks * 8, width), dtype),
        grid_spec=pltpu.PrefetchScalarGridSpec(
            num_scalar_prefetch=3,
            grid=(tiles // per_step,),
            in_specs=[
                pl.BlockSpec(held.shape, lambda i, *_: (0, 0, 0)),
                spec,
                spec,
            ],
            out_specs=pl.BlockSpec((blocks * 8, width), lambda i, *_: (0, 0)),
            scratch_shapes=[pltpu.VMEM((blocks, 8, width), F32)],
        ),
        compiler_params=pltpu.CompilerParams(vmem_limit_bytes=VMEM_LIMIT),
        cost_estimate=pl.CostEstimate(
            flops=4 * tiles * GROUP * 8 * rank_max * width,
            bytes_accessed=4 * tiles * rank_max * width,
            transcendentals=0,
        ),
    )(take, put, ranks, held, first, second)


def stations_kernel(
    pairs, weight, part, out,
    got_c, send_line, got_line, own,
    c_send, c_recv, l_send, l_recv, a_send, a_recv, t_send, t_recv, local_sem
):
    me = lax.axis_index("tile")
    core = lax.rem(me, 2)
    pair = me // 2
    twin = pair * 2 + 1 - core
    chunk = part.shape[0] // (2 * pairs)

    def peer(d):
        return lax.rem(pair + d, pairs) * 2 + core

    def band(c, d):
        where = c * pairs + lax.rem(pair + d, pairs)
        return pl.ds(pl.multiple_of(where * chunk, chunk), chunk)

    barrier = pltpu.get_barrier_semaphore()
    for d in range(1, pairs):
        pl.semaphore_signal(barrier, inc=1, device_id={"tile": peer(d)}, device_id_type=MESH)
    pl.semaphore_signal(barrier, inc=1, device_id={"tile": twin}, device_id_type=MESH)
    pl.semaphore_wait(barrier, pairs)

    order = list(range(1, pairs)) + [0]
    copies, lines = [], []
    for d in order:
        copy = remote(
            part.at[band(1 - core, d)], got_c.at[d], c_send.at[d], c_recv.at[d], twin
        )
        copy.start()
        copies.append(copy)
    for d, copy in zip(order, copies):
        copy.wait_recv()
        value = part[band(core, d)] + got_c[d]
        if d:
            send_line[d - 1] = value.astype(BF16)
            line = remote(
                send_line.at[d - 1], got_line.at[d - 1], l_send.at[d - 1], l_recv.at[d - 1],
                peer(d),
            )
            line.start()
            lines.append(line)
        else:
            total = value
    for d in range(1, pairs):
        lines[d - 1].wait_recv()
        total += got_line[d - 1].astype(F32)
    count = own.shape[0]
    width = part.shape[1]
    for b in range(count):
        start = pl.multiple_of(me * (count * width) + b * width, width)
        factor = weight[:, pl.ds(start, width)]
        own[b] = halves(total[b * 8 : (b + 1) * 8] * factor).astype(BF16)
    sent = []

    def go(src, slot, send, recv, target):
        copy = remote(src, out.at[slot], send, recv, target)
        copy.start()
        sent.append(copy)

    for d in range(1, pairs):
        go(own, me, a_send.at[d - 1], a_recv.at[d - 1], peer(d))
    go(own, me, t_send.at[0], t_recv.at[0], twin)
    mine = pltpu.make_async_copy(own, out.at[me], local_sem)
    mine.start()
    for d in range(1, pairs):
        slot = peer(pairs - d)
        remote(own, out.at[slot], a_send.at[d - 1], a_recv.at[d - 1], slot).wait_recv()
        go(out.at[slot], slot, t_send.at[d], t_recv.at[d], twin)
    for d in range(pairs):
        slot = lax.rem(pair + pairs - d, pairs) * 2 + 1 - core
        remote(own, out.at[slot], t_send.at[d], t_recv.at[d], twin).wait_recv()
    mine.wait()
    for copy in copies + lines + sent:
        copy.wait_send()


def back_kernel(
    lines, units, contrast, level, label, part, out,
    got_c, send_y, got_y, send_z, got_z,
    c_send, c_recv, y_send, y_recv, z_send, z_recv
):
    _, core, side, step = place(lines)
    across = index_of(step, 1 - side, core)
    twin = index_of(step, side, 1 - core)
    enter(lines, step, side, core)
    chunk = part.shape[0] // (4 * lines)

    def band(c, y, z):
        return pl.ds(pl.multiple_of(((c * 2 + y) * lines + z) * chunk, chunk), chunk)

    def target(k):
        return lax.rem(step + k + 1, lines)

    c_copies = [[None] * lines, [None] * lines]
    for k in range(lines):
        for far in range(2):
            y = 1 - side if far == 0 else side
            copy = remote(
                part.at[band(1 - core, y, target(k))],
                got_c.at[far, k],
                c_send.at[far, k],
                c_recv.at[far, k],
                twin,
            )
            copy.start()
            c_copies[far][k] = copy
    y_copies = []
    for k in range(lines):
        c_copies[0][k].wait_recv()
        send_y[k] = (
            part[band(core, 1 - side, target(k))].astype(F32) + got_c[0, k].astype(F32)
        ).astype(BF16)
        copy = remote(send_y.at[k], got_y.at[k], y_send.at[k], y_recv.at[k], across)
        copy.start()
        y_copies.append(copy)
    z_copies = []
    total = None
    for k in range(lines):
        c_copies[1][k].wait_recv()
        y_copies[k].wait_recv()
        value = (
            part[band(core, side, target(k))].astype(F32)
            + got_c[1, k].astype(F32)
            + got_y[k].astype(F32)
        )
        if k < lines - 1:
            send_z[k] = value.astype(BF16)
            copy = remote(
                send_z.at[k], got_z.at[k], z_send.at[k], z_recv.at[k],
                index_of(target(k), side, core),
            )
            copy.start()
            z_copies.append(copy)
        else:
            total = value
    for copy in z_copies:
        copy.wait_recv()
    width = part.shape[1]
    for b in range(chunk // 8):
        rows = slice(b * 8, (b + 1) * 8)
        cut = pl.ds(b * width, width)
        piece = total[rows]
        for k in range(lines - 1):
            piece += got_z[k, b * 8 : (b + 1) * 8].astype(F32)
        out[:, cut] = piece * cell_scaling(level[:, cut], label[:, cut], contrast, units)
    for copy in c_copies[0] + c_copies[1] + y_copies + z_copies:
        copy.wait_send()


def params(number):
    return pltpu.CompilerParams(
        collective_id=number, has_side_effects=True, vmem_limit_bytes=VMEM_LIMIT
    )


VM = pl.BlockSpec(memory_space=pltpu.VMEM)
SM = pl.BlockSpec(memory_space=pltpu.SMEM)
ANY = pl.BlockSpec(memory_space=pl.ANY)


def shards(
    probes,
    level_set,
    unit_label,
    contrast,
    station_weight,
    u_factor,
    v_factor,
    col_owner,
    col_local,
    row_owner,
    row_local,
    tile_rank,
):
    peers = lax.axis_size("tile")
    lines = peers // 4
    own_index = lax.axis_index("tile")
    tiles, rank_max, width = u_factor.shape
    cell_total = probes.shape[1]
    cell_blocks = cell_total // width
    station_blocks = station_weight.shape[0] // (peers * width)
    units = contrast.shape[0]
    half = width // 2
    dma = pltpu.SemaphoreType.DMA

    def own_part(table):
        return lax.dynamic_slice_in_dim(table.reshape(-1), own_index * tiles, tiles)

    def places(owner, local, blocks, by_side):
        owner, local = own_part(owner), own_part(local)
        if by_side:
            moved = (owner % 2 * 2 + owner // 2 % 2) * lines + owner // 4
        else:
            moved = owner % 2 * (peers // 2) + owner // 2
        return owner * blocks + local, moved * blocks + local

    col_take, col_put = places(col_owner, col_local, cell_blocks, True)
    row_take, row_put = places(row_owner, row_local, station_blocks, False)
    ranks = own_part(tile_rank)
    u_rows = u_factor.reshape(tiles * rank_max, width)
    v_rows = v_factor.reshape(tiles * rank_max, width)
    level = level_set.reshape(1, cell_total)
    label = unit_label.reshape(1, cell_total)
    weight = station_weight.reshape(1, -1)

    with jax.named_scope("gather_cells"):
        cells = pl.pallas_call(
            functools.partial(cells_kernel, lines, units),
            out_shape=jax.ShapeDtypeStruct((peers, cell_blocks, 16, half), BF16),
            in_specs=[SM, VM, VM, VM],
            out_specs=ANY,
            scratch_shapes=[pltpu.VMEM((cell_blocks, 16, half), BF16), dma]
            + gather_sems(lines),
            compiler_params=params(0),
        )(contrast, probes, level, label)

    with jax.named_scope("forward_tiles"):
        partial = apply_tiles(
            col_take, row_put, ranks, cells.reshape(-1, 16, half), v_rows, u_rows,
            peers * station_blocks, F32, rank_max,
        )

    chunk = station_blocks * 8
    pairs = peers // 2
    with jax.named_scope("sum_stations"):
        data = pl.pallas_call(
            functools.partial(stations_kernel, pairs),
            out_shape=jax.ShapeDtypeStruct((peers, station_blocks, 16, half), BF16),
            in_specs=[VM, VM],
            out_specs=ANY,
            scratch_shapes=[
                pltpu.VMEM((pairs, chunk, width), F32),
                pltpu.VMEM((pairs - 1, chunk, width), BF16),
                pltpu.VMEM((pairs - 1, chunk, width), BF16),
                pltpu.VMEM((station_blocks, 16, half), BF16),
                dma((pairs,)),
                dma((pairs,)),
                dma((pairs - 1,)),
                dma((pairs - 1,)),
                dma((pairs - 1,)),
                dma((pairs - 1,)),
                dma((pairs,)),
                dma((pairs,)),
                dma,
            ],
            compiler_params=params(1),
        )(weight, partial)

    with jax.named_scope("adjoint_tiles"):
        spread = apply_tiles(
            row_take, col_put, ranks, data.reshape(-1, 16, half), u_rows, v_rows,
            peers * cell_blocks, BF16, rank_max,
        )

    chunk = cell_blocks * 8
    with jax.named_scope("sum_cells"):
        return pl.pallas_call(
            functools.partial(back_kernel, lines, units),
            out_shape=jax.ShapeDtypeStruct(probes.shape, F32),
            in_specs=[SM, VM, VM, VM],
            out_specs=VM,
            scratch_shapes=[
                pltpu.VMEM((2, lines, chunk, width), BF16),
                pltpu.VMEM((lines, chunk, width), BF16),
                pltpu.VMEM((lines, chunk, width), BF16),
                pltpu.VMEM((lines - 1, chunk, width), BF16),
                pltpu.VMEM((lines - 1, chunk, width), BF16),
                dma((2, lines)),
                dma((2, lines)),
                dma((lines,)),
                dma((lines,)),
                dma((lines - 1,)),
                dma((lines - 1,)),
            ],
            compiler_params=params(2),
        )(contrast, level, label, spread)


def solution(mesh):
    placed = (
        P(None, ("groups", "tile")),
        P(("groups", "tile")),
        P(("groups", "tile")),
        P("groups"),
        P("groups"),
        P(("groups", "tile"), None, None),
        P(("groups", "tile"), None, None),
        P("groups", None),
        P("groups"),
        P("groups", None),
        P("groups"),
        P("groups"),
    )
    return jax.shard_map(
        shards, mesh=mesh, in_specs=placed, out_specs=P(None, ("groups", "tile")), check_vma=False
    )
```

profile of v0, /device:TPU:0, one launch (start us, length us, event | category | flops | bytes accessed | tf_op | source)
XLA Modules:
  0.0 92.6 jit_solution(17471492028878166664)
XLA Ops:
  0.0 1.3 %dynamic_slice.25.ranks = s32[128]{0:T(128)} dynamic-slice(s32[2048]{0:T(1024)} %param.23, s32[]{:T(128)S(6)} %select_n.33), dynamic_slice_sizes={128} | dynamic-slice | bytes 1028 | tf_op jit(solution)/shard_map/dynamic_slice | solution.py:396
  1.3 1.4 %fusion.5 = (s32[128]{0:T(128)}, s32[128]{0:T(128)}, s32[128]{0:T(128)}, s32[128]{0:T(128)}) fusion(s32[2048,1]{0,1:T(1,128)} %param.19, s32[]{:T(128)S(6)} %select_n.33, s32[2048]{0:T(1024)} %param.20, s32[2048]{0:T(1024)} %param.22, s32[2048,1]{0,1:T(1,128)} %param.21), kind=kLoop, calls=%fused_computation.24 | loop fusion | flops 9344 | bytes 4100 | tf_op jit(solution)/shard_map/add | solution.py:404
  2.6 25.2 %gather_cells.1 = bf16[16,16,16,256]{3,2,1,0:T(8,128)(2,1)} custom-call(f32[4]{0:T(128)} %contrast.3, f32[8,8192]{1,0:T(8,128)} %probes.1, f32[1,8192]{1,0:T(1,128)} %bitcast.50, s32[1,8192]{1,0:T(1,128)} %bitcast.52), custom_call_target="tpu_custom_call" | custom-call | tf_op jit(solution)/shard_map/gather_cells/pallas_call | solution.py:416
  27.8 7.8 %forward_tiles.1.part = f32[512,512]{1,0:T(8,128)} custom-call(s32[128]{0:T(128)} %get-tuple-element.7.take, s32[128]{0:T(128)} %get-tuple-element.10.put, s32[128]{0:T(128)} %dynamic_slice.25.ranks, bf16[256,16,256]{2,1,0:T(8,128)(2,1)} %bitcast.48, bf16[4096,512]{1,0:T(8,128)(2,1)} %bitcast.44, bf16[4096,512]{1,0:T(8,128)(2,1)} %bitcast.46), custom_call_target="tpu_custom_call" | custom-call | flops 536870912 | bytes 8388608 | tf_op jit(solution)/shard_map/forward_tiles/pallas_call | solution.py:185
  35.6 21.9 %sum_stations.1 = bf16[16,4,16,256]{3,2,1,0:T(8,128)(2,1)} custom-call(f32[1,32768]{1,0:T(1,128)} %bitcast.54, f32[512,512]{1,0:T(8,128)} %forward_tiles.1.part), custom_call_target="tpu_custom_call" | custom-call | tf_op jit(solution)/shard_map/sum_stations/pallas_call | solution.py:435
  57.5 7.9 %adjoint_tiles.1.part = bf16[2048,512]{1,0:T(8,128)(2,1)} custom-call(s32[128]{0:T(128)} %get-tuple-element.9.take, s32[128]{0:T(128)} %get-tuple-element.8.put, s32[128]{0:T(128)} %dynamic_slice.25.ranks, bf16[64,16,256]{2,1,0:T(8,128)(2,1)} %bitcast.49, bf16[4096,512]{1,0:T(8,128)(2,1)} %bitcast.47, bf16[4096,512]{1,0:T(8,128)(2,1)} %bitcast.45), custom_call_target="tpu_custom_call" | custom-call | flops 536870912 | bytes 8388608 | tf_op jit(solution)/shard_map/adjoint_tiles/pallas_call | solution.py:185
  65.4 25.5 %sum_cells.1 = f32[8,8192]{1,0:T(8,128)} custom-call(f32[4]{0:T(128)} %contrast.3, f32[1,8192]{1,0:T(1,128)} %bitcast.51, s32[1,8192]{1,0:T(1,128)} %bitcast.53, bf16[2048,512]{1,0:T(8,128)(2,1)} %adjoint_tiles.1.part), custom_call_target="tpu_custom_call" | custom-call | tf_op jit(solution)/shard_map/sum_cells/pallas_call | solution.py:466
  90.9 1.7 %copy.14 = f32[8,8192]{1,0:T(8,128)} copy(f32[8,8192]{1,0:T(8,128)} %sum_cells.1) | data formatting | bytes 524288
where the time goes:
time: 92.9 us; the launch traced here: 92.6 us
  Pallas kernels  88.2 us (95%)
  local copies, waits for them, and re-layouts  2.93 us (3%)
  other arithmetic  1.38 us (1%)
    pallas_call x1, Pallas kernels, shards(): pl.pallas_call(functools.partial(back_kernel, lines, units), out_shape=ja...  25.5 us
    pallas_call x1, Pallas kernels, shards(): pl.pallas_call(functools.partial(cells_kernel, lines, units), out_shape=j...  25.2 us
    pallas_call x1, Pallas kernels, shards(): pl.pallas_call(functools.partial(stations_kernel, pairs), out_shape=jax.S...  21.9 us
    pallas_call x2, Pallas kernels, apply_tiles(): pl.pallas_call(functools.partial(tiles_kernel, per_step, rank_max), out_s...  15.6 us

commit v1 on v0

--- a/solution.py
+++ b/solution.py
@@ -47,59 +47,74 @@
     )
 
 
-def gather_shards(lines, own, out, local_sem, sems, step, side, core):
+def gather_shards(lines, parts, fill, own, out, local_sem, sems, step, side, core):
     send_z, recv_z, send_y, recv_y, send_c, recv_c = sems
     me = index_of(step, side, core)
     across = index_of(step, 1 - side, core)
     twin = index_of(step, side, 1 - core)
+    size = own.shape[0] // parts
     started = []
 
-    def go(src, slot, send, recv, peer):
-        copy = remote(src, out.at[slot], send, recv, peer)
+    def at(slot, p):
+        return out.at[slot, pl.ds(p * size, size)]
+
+    def go(src, slot, p, send, recv, peer):
+        copy = remote(src, at(slot, p), send, recv, peer)
         copy.start()
         started.append(copy)
 
-    go(own, me, send_y.at[0], recv_y.at[0], across)
-    for d in range(1, lines):
-        peer = index_of(lax.rem(step + d, lines), side, core)
-        go(own, me, send_z.at[d - 1], recv_z.at[d - 1], peer)
-    go(own, me, send_c.at[0], recv_c.at[0], twin)
+    def arrived(slot, p, recv, peer):
+        remote(at(slot, p), at(slot, p), recv, recv, peer).wait_recv()
+
+    for p in range(parts):
+        fill(p)
+        piece = own.at[pl.ds(p * size, size)]
+        go(piece, me, p, send_y.at[0, p], recv_y.at[0, p], across)
+        for d in range(1, lines):
+            peer = index_of(lax.rem(step + d, lines), side, core)
+            go(piece, me, p, send_z.at[d - 1, p], recv_z.at[d - 1, p], peer)
+    for p in range(parts):
+        piece = own.at[pl.ds(p * size, size)]
+        go(piece, me, p, send_c.at[0, p], recv_c.at[0, p], twin)
     mine = pltpu.make_async_copy(own, out.at[me], local_sem)
     mine.start()
 
-    def arrived(slot, recv, peer):
-        remote(out.at[slot], out.at[slot], recv, recv, peer).wait_recv()
-
-    for k in range(lines + 1):
-        if 1 <= k < lines:
-            slot = index_of(lax.rem(step + lines - k, lines), side, core)
-            arrived(slot, recv_z.at[k - 1], me)
-            go(out.at[slot], slot, send_y.at[k], recv_y.at[k], across)
-            go(out.at[slot], slot, send_c.at[k], recv_c.at[k], twin)
-        if k >= 1:
-            j = k - 1
-            slot = index_of(lax.rem(step + lines - j, lines), 1 - side, core)
-            arrived(slot, recv_y.at[j], across)
-            go(out.at[slot], slot, send_c.at[lines + j], recv_c.at[lines + j], twin)
-    for k in range(lines):
-        for far in range(2):
-            where = 1 - side if far else side
-            slot = index_of(lax.rem(step + lines - k, lines), where, 1 - core)
-            arrived(slot, recv_c.at[far * lines + k], twin)
+    for p in range(parts + 1):
+        if p < parts:
+            for k in range(1, lines):
+                slot = index_of(lax.rem(step + lines - k, lines), side, core)
+                arrived(slot, p, recv_z.at[k - 1, p], me)
+                go(at(slot, p), slot, p, send_y.at[k, p], recv_y.at[k, p], across)
+                go(at(slot, p), slot, p, send_c.at[k, p], recv_c.at[k, p], twin)
+        if p >= 1:
+            for k in range(lines):
+                slot = index_of(lax.rem(step + lines - k, lines), 1 - side, core)
+                arrived(slot, p - 1, recv_y.at[k, p - 1], across)
+                far = lines + k
+                go(
+                    at(slot, p - 1), slot, p - 1,
+                    send_c.at[far, p - 1], recv_c.at[far, p - 1], twin,
+                )
+    for p in range(parts):
+        for k in range(lines):
+            for far in range(2):
+                where = 1 - side if far else side
+                slot = index_of(lax.rem(step + lines - k, lines), where, 1 - core)
+                arrived(slot, p, recv_c.at[far * lines + k, p], twin)
     mine.wait()
     for copy in started:
         copy.wait_send()
 
 
-def gather_sems(lines):
+def gather_sems(lines, parts):
     dma = pltpu.SemaphoreType.DMA
     return [
-        dma((lines - 1,)),
-        dma((lines - 1,)),
-        dma((lines,)),
-        dma((lines,)),
-        dma((2 * lines,)),
-        dma((2 * lines,)),
+        dma((lines - 1, parts)),
+        dma((lines - 1, parts)),
+        dma((lines, parts)),
+        dma((lines, parts)),
+        dma((2 * lines, parts)),
+        dma((2 * lines, parts)),
     ]
 
 
@@ -115,16 +130,22 @@
     return jnp.concatenate([block[:, :half], block[:, half:]], axis=0)
 
 
-def cells_kernel(lines, units, contrast, probes, level, label, out, own, local_sem, *sems):
+def cells_kernel(
+    lines, units, parts, contrast, probes, level, label, out, own, local_sem, *sems
+):
     _, core, side, step = place(lines)
-    enter(lines, step, side, core)
     count = own.shape[0]
     width = probes.shape[1] // count
-    for b in range(count):
-        cut = pl.ds(b * width, width)
-        scaling = cell_scaling(level[:, cut], label[:, cut], contrast, units)
-        own[b] = halves(probes[:, cut] * scaling).astype(BF16)
-    gather_shards(lines, own, out, local_sem, sems, step, side, core)
+    size = count // parts
+
+    def fill(p):
+        for b in range(p * size, (p + 1) * size):
+            cut = pl.ds(b * width, width)
+            scaling = cell_scaling(level[:, cut], label[:, cut], contrast, units)
+            own[b] = halves(probes[:, cut] * scaling).astype(BF16)
+
+    enter(lines, step, side, core)
+    gather_shards(lines, parts, fill, own, out, local_sem, sems, step, side, core)
 
 
 def tiles_kernel(
@@ -390,6 +411,7 @@
     station_blocks = station_weight.shape[0] // (peers * width)
     units = contrast.shape[0]
     half = width // 2
+    parts = 4 if cell_blocks % 4 == 0 else 1
     dma = pltpu.SemaphoreType.DMA
 
     def own_part(table):
@@ -414,12 +436,12 @@
 
     with jax.named_scope("gather_cells"):
         cells = pl.pallas_call(
-            functools.partial(cells_kernel, lines, units),
+            functools.partial(cells_kernel, lines, units, parts),
             out_shape=jax.ShapeDtypeStruct((peers, cell_blocks, 16, half), BF16),
             in_specs=[SM, VM, VM, VM],
             out_specs=ANY,
             scratch_shapes=[pltpu.VMEM((cell_blocks, 16, half), BF16), dma]
-            + gather_sems(lines),
+            + gather_sems(lines, parts),
             compiler_params=params(0),
         )(contrast, probes, level, label)
 

time: 92.9 us -> 93.3 us (level)
  no operation moved by 1% of the time
where the time goes in v1:
time: 93.3 us; the launch traced here: 92.9 us
  Pallas kernels  88.6 us (95%)
  local copies, waits for them, and re-layouts  2.93 us (3%)
  other arithmetic  1.38 us (1%)
    pallas_call x1, Pallas kernels, shards(): pl.pallas_call(functools.partial(cells_kernel, lines, units, parts), out_...  25.7 us
    pallas_call x1, Pallas kernels, shards(): pl.pallas_call(functools.partial(back_kernel, lines, units), out_shape=ja...  25.4 us
    pallas_call x1, Pallas kernels, shards(): pl.pallas_call(functools.partial(stations_kernel, pairs), out_shape=jax.S...  21.9 us
    pallas_call x2, Pallas kernels, apply_tiles(): pl.pallas_call(functools.partial(tiles_kernel, per_step, rank_max), out_s...  15.6 us

profile of v1, /device:TPU:0, one launch (start us, length us, event | category | flops | bytes accessed | tf_op | source)
XLA Modules:
  0.0 92.9 jit_solution(9328590821893523213)
XLA Ops:
  0.0 1.3 %dynamic_slice.25.ranks = s32[128]{0:T(128)} dynamic-slice(s32[2048]{0:T(1024)} %param.23, s32[]{:T(128)S(6)} %select_n.33), dynamic_slice_sizes={128} | dynamic-slice | bytes 1028 | tf_op jit(solution)/shard_map/dynamic_slice | solution.py:418
  1.3 1.4 %fusion.5 = (s32[128]{0:T(128)}, s32[128]{0:T(128)}, s32[128]{0:T(128)}, s32[128]{0:T(128)}) fusion(s32[2048,1]{0,1:T(1,128)} %param.19, s32[]{:T(128)S(6)} %select_n.33, s32[2048]{0:T(1024)} %param.20, s32[2048]{0:T(1024)} %param.22, s32[2048,1]{0,1:T(1,128)} %param.21), kind=kLoop, calls=%fused_computation.24 | loop fusion | flops 9344 | bytes 4100 | tf_op jit(solution)/shard_map/add | solution.py:426
  2.6 25.7 %gather_cells.1 = bf16[16,16,16,256]{3,2,1,0:T(8,128)(2,1)} custom-call(f32[4]{0:T(128)} %contrast.3, f32[8,8192]{1,0:T(8,128)} %probes.1, f32[1,8192]{1,0:T(1,128)} %bitcast.50, s32[1,8192]{1,0:T(1,128)} %bitcast.52), custom_call_target="tpu_custom_call" | custom-call | tf_op jit(solution)/shard_map/gather_cells/pallas_call | solution.py:438
  28.4 7.7 %forward_tiles.1.part = f32[512,512]{1,0:T(8,128)} custom-call(s32[128]{0:T(128)} %get-tuple-element.7.take, s32[128]{0:T(128)} %get-tuple-element.10.put, s32[128]{0:T(128)} %dynamic_slice.25.ranks, bf16[256,16,256]{2,1,0:T(8,128)(2,1)} %bitcast.48, bf16[4096,512]{1,0:T(8,128)(2,1)} %bitcast.44, bf16[4096,512]{1,0:T(8,128)(2,1)} %bitcast.46), custom_call_target="tpu_custom_call" | custom-call | flops 536870912 | bytes 8388608 | tf_op jit(solution)/shard_map/forward_tiles/pallas_call | solution.py:206
  36.1 21.9 %sum_stations.1 = bf16[16,4,16,256]{3,2,1,0:T(8,128)(2,1)} custom-call(f32[1,32768]{1,0:T(1,128)} %bitcast.54, f32[512,512]{1,0:T(8,128)} %forward_tiles.1.part), custom_call_target="tpu_custom_call" | custom-call | tf_op jit(solution)/shard_map/sum_stations/pallas_call | solution.py:457
  58.0 7.9 %adjoint_tiles.1.part = bf16[2048,512]{1,0:T(8,128)(2,1)} custom-call(s32[128]{0:T(128)} %get-tuple-element.9.take, s32[128]{0:T(128)} %get-tuple-element.8.put, s32[128]{0:T(128)} %dynamic_slice.25.ranks, bf16[64,16,256]{2,1,0:T(8,128)(2,1)} %bitcast.49, bf16[4096,512]{1,0:T(8,128)(2,1)} %bitcast.47, bf16[4096,512]{1,0:T(8,128)(2,1)} %bitcast.45), custom_call_target="tpu_custom_call" | custom-call | flops 536870912 | bytes 8388608 | tf_op jit(solution)/shard_map/adjoint_tiles/pallas_call | solution.py:206
  65.9 25.4 %sum_cells.1 = f32[8,8192]{1,0:T(8,128)} custom-call(f32[4]{0:T(128)} %contrast.3, f32[1,8192]{1,0:T(1,128)} %bitcast.51, s32[1,8192]{1,0:T(1,128)} %bitcast.53, bf16[2048,512]{1,0:T(8,128)(2,1)} %adjoint_tiles.1.part), custom_call_target="tpu_custom_call" | custom-call | tf_op jit(solution)/shard_map/sum_cells/pallas_call | solution.py:488
  91.3 1.7 %copy.14 = f32[8,8192]{1,0:T(8,128)} copy(f32[8,8192]{1,0:T(8,128)} %sum_cells.1) | data formatting | bytes 524288

commit v2 on v1

--- a/solution.py
+++ b/solution.py
@@ -226,7 +226,7 @@
     )(take, put, ranks, held, first, second)
 
 
-def stations_kernel(
+def stations_phase(
     pairs, weight, part, out,
     got_c, send_line, got_line, own,
     c_send, c_recv, l_send, l_recv, a_send, a_recv, t_send, t_recv, local_sem
@@ -236,6 +236,8 @@
     pair = me // 2
     twin = pair * 2 + 1 - core
     chunk = part.shape[0] // (2 * pairs)
+    count = own.shape[0]
+    width = part.shape[1]
 
     def peer(d):
         return lax.rem(pair + d, pairs) * 2 + core
@@ -244,11 +246,8 @@
         where = c * pairs + lax.rem(pair + d, pairs)
         return pl.ds(pl.multiple_of(where * chunk, chunk), chunk)
 
-    barrier = pltpu.get_barrier_semaphore()
-    for d in range(1, pairs):
-        pl.semaphore_signal(barrier, inc=1, device_id={"tile": peer(d)}, device_id_type=MESH)
-    pl.semaphore_signal(barrier, inc=1, device_id={"tile": twin}, device_id_type=MESH)
-    pl.semaphore_wait(barrier, pairs)
+    def shard(slot):
+        return out.at[pl.ds(slot * count, count)]
 
     order = list(range(1, pairs)) + [0]
     copies, lines = [], []
@@ -274,8 +273,6 @@
     for d in range(1, pairs):
         lines[d - 1].wait_recv()
         total += got_line[d - 1].astype(F32)
-    count = own.shape[0]
-    width = part.shape[1]
     for b in range(count):
         start = pl.multiple_of(me * (count * width) + b * width, width)
         factor = weight[:, pl.ds(start, width)]
@@ -283,98 +280,166 @@
     sent = []
 
     def go(src, slot, send, recv, target):
-        copy = remote(src, out.at[slot], send, recv, target)
+        copy = remote(src, shard(slot), send, recv, target)
         copy.start()
         sent.append(copy)
 
     for d in range(1, pairs):
         go(own, me, a_send.at[d - 1], a_recv.at[d - 1], peer(d))
     go(own, me, t_send.at[0], t_recv.at[0], twin)
-    mine = pltpu.make_async_copy(own, out.at[me], local_sem)
+    mine = pltpu.make_async_copy(own, shard(me), local_sem)
     mine.start()
     for d in range(1, pairs):
         slot = peer(pairs - d)
-        remote(own, out.at[slot], a_send.at[d - 1], a_recv.at[d - 1], slot).wait_recv()
-        go(out.at[slot], slot, t_send.at[d], t_recv.at[d], twin)
+        remote(own, shard(slot), a_send.at[d - 1], a_recv.at[d - 1], slot).wait_recv()
+        go(shard(slot), slot, t_send.at[d], t_recv.at[d], twin)
     for d in range(pairs):
         slot = lax.rem(pair + pairs - d, pairs) * 2 + 1 - core
-        remote(own, out.at[slot], t_send.at[d], t_recv.at[d], twin).wait_recv()
+        remote(own, shard(slot), t_send.at[d], t_recv.at[d], twin).wait_recv()
     mine.wait()
-    for copy in copies + lines + sent:
-        copy.wait_send()
-
-
-def back_kernel(
-    lines, units, contrast, level, label, part, out,
-    got_c, send_y, got_y, send_z, got_z,
-    c_send, c_recv, y_send, y_recv, z_send, z_recv
+    return copies + lines + sent
+
+
+def adjoint_kernel(
+    lines, units, capacity, rank_max,
+    contrast, slot_tile, slot_row, slot_rank, target_row, level, label, weight, part, u_hbm, v_hbm,
+    out,
+    u_here, v_here, data,
+    got_c, send_line, got_line, own,
+    send_twin, got_twin, send_y, got_y, near, send_z, got_z,
+    c_send, c_recv, l_send, l_recv, a_send, a_recv, t_send, t_recv, local_sem, u_sem, v_sem,
+    x_send, x_recv, y_send, y_recv, z_send, z_recv
 ):
-    _, core, side, step = place(lines)
+    me, core, side, step = place(lines)
+    pairs = 2 * lines
     across = index_of(step, 1 - side, core)
     twin = index_of(step, side, 1 - core)
-    enter(lines, step, side, core)
-    chunk = part.shape[0] // (4 * lines)
-
-    def band(c, y, z):
-        return pl.ds(pl.multiple_of(((c * 2 + y) * lines + z) * chunk, chunk), chunk)
+    barrier = pltpu.get_barrier_semaphore()
+    for d in range(1, pairs):
+        peer = lax.rem(me // 2 + d, pairs) * 2 + core
+        pl.semaphore_signal(barrier, inc=1, device_id={"tile": peer}, device_id_type=MESH)
+    pl.semaphore_signal(barrier, inc=1, device_id={"tile": twin}, device_id_type=MESH)
+    u_copy = pltpu.make_async_copy(u_hbm, u_here, u_sem)
+    v_copy = pltpu.make_async_copy(v_hbm, v_here, v_sem)
+    u_copy.start()
+    v_copy.start()
+    pl.semaphore_wait(barrier, pairs)
+    pending = stations_phase(
+        pairs, weight, part, data,
+        got_c, send_line, got_line, own,
+        c_send, c_recv, l_send, l_recv, a_send, a_recv, t_send, t_recv, local_sem,
+    )
+    u_copy.wait()
+    v_copy.wait()
+
+    size = min(GROUP, capacity)
+    groups = capacity // size
+    rows = size * rank_max
+    chunk = near.shape[1]
+    lane = lax.broadcasted_iota(jnp.int32, (8, rows), 1)
+    line = lax.broadcasted_iota(jnp.int32, (chunk, size * 8), 0)
+
+    def chunks(owners):
+        jobs = [(o, g) for o in owners for g in range(groups)]
+        inners = []
+        for o, g in jobs:
+            pieces, factors = [], []
+            for j in range(size):
+                s = o * capacity + g * size + j
+                block = data[slot_row[s]].astype(F32)
+                pieces.append(jnp.concatenate([block[:8], block[8:]], axis=1))
+                factors.append(u_here[slot_tile[s]])
+            inners.append(
+                lax.dot_general(
+                    jnp.concatenate(pieces, axis=0).astype(BF16),
+                    jnp.concatenate(factors, axis=0),
+                    (((1,), (1,)), ((), ())),
+                    preferred_element_type=F32,
+                )
+            )
+        spread = []
+        for (o, g), inner in zip(jobs, inners):
+            kept = []
+            for j in range(size):
+                start = j * rank_max
+                end = start + slot_rank[o * capacity + g * size + j]
+                piece = inner[j * 8 : (j + 1) * 8]
+                kept.append(jnp.where((lane >= start) & (lane < end), piece, 0.0))
+            kept = jnp.concatenate(kept, axis=0).astype(BF16)
+            chosen = jnp.where(line == target_row[o * groups + g], 1.0, 0.0).astype(BF16)
+            spread.append(jnp.dot(chosen, kept, preferred_element_type=F32).astype(BF16))
+        values = []
+        for n in range(len(owners)):
+            value = None
+            for g in range(groups):
+                s = owners[n] * capacity + g * size
+                factors = jnp.concatenate([v_here[slot_tile[s + j]] for j in range(size)], axis=0)
+                term = jnp.dot(spread[n * groups + g], factors, preferred_element_type=F32)
+                value = term if value is None else value + term
+            values.append(value)
+        return values
 
     def target(k):
         return lax.rem(step + k + 1, lines)
 
-    c_copies = [[None] * lines, [None] * lines]
-    for k in range(lines):
-        for far in range(2):
-            y = 1 - side if far == 0 else side
-            copy = remote(
-                part.at[band(1 - core, y, target(k))],
-                got_c.at[far, k],
-                c_send.at[far, k],
-                c_recv.at[far, k],
-                twin,
-            )
-            copy.start()
-            c_copies[far][k] = copy
-    y_copies = []
-    for k in range(lines):
-        c_copies[0][k].wait_recv()
-        send_y[k] = (
-            part[band(core, 1 - side, target(k))].astype(F32) + got_c[0, k].astype(F32)
-        ).astype(BF16)
-        copy = remote(send_y.at[k], got_y.at[k], y_send.at[k], y_recv.at[k], across)
-        copy.start()
-        y_copies.append(copy)
-    z_copies = []
-    total = None
-    for k in range(lines):
-        c_copies[1][k].wait_recv()
-        y_copies[k].wait_recv()
-        value = (
-            part[band(core, side, target(k))].astype(F32)
-            + got_c[1, k].astype(F32)
-            + got_y[k].astype(F32)
-        )
-        if k < lines - 1:
-            send_z[k] = value.astype(BF16)
-            copy = remote(
-                send_z.at[k], got_z.at[k], z_send.at[k], z_recv.at[k],
-                index_of(target(k), side, core),
-            )
-            copy.start()
-            z_copies.append(copy)
-        else:
-            total = value
-    for copy in z_copies:
-        copy.wait_recv()
+    def twin_copy(far, k):
+        return remote(
+            send_twin.at[far, k], got_twin.at[far, k], x_send.at[far, k], x_recv.at[far, k], twin
+        )
+
+    def y_copy(k):
+        return remote(send_y.at[k], got_y.at[k], y_send.at[k], y_recv.at[k], across)
+
+    def z_copy(k):
+        return remote(
+            send_z.at[k], got_z.at[k], z_send.at[k], z_recv.at[k],
+            index_of(target(k), side, core),
+        )
+
+    def one_target(k, _):
+        there = target(k)
+        first, second = chunks(
+            [index_of(there, 1 - side, 1 - core), index_of(there, side, 1 - core)]
+        )
+        send_twin[0, k] = first.astype(BF16)
+        twin_copy(0, k).start()
+        send_twin[1, k] = second.astype(BF16)
+        twin_copy(1, k).start()
+        first, second = chunks([index_of(there, 1 - side, core), index_of(there, side, core)])
+        twin_copy(0, k).wait_recv()
+        send_y[k] = (first + got_twin[0, k].astype(F32)).astype(BF16)
+        y_copy(k).start()
+        twin_copy(1, k).wait_recv()
+        near[k] = second + got_twin[1, k].astype(F32)
+
+        @pl.when(k > 0)
+        def _():
+            y_copy(k - 1).wait_recv()
+            send_z[k - 1] = (near[k - 1] + got_y[k - 1].astype(F32)).astype(BF16)
+            z_copy(k - 1).start()
+
+        return 0
+
+    lax.fori_loop(0, lines, one_target, 0)
+    y_copy(lines - 1).wait_recv()
+    for k in range(lines - 1):
+        z_copy(k).wait_recv()
     width = part.shape[1]
     for b in range(chunk // 8):
-        rows = slice(b * 8, (b + 1) * 8)
         cut = pl.ds(b * width, width)
-        piece = total[rows]
+        band = slice(b * 8, (b + 1) * 8)
+        piece = near[lines - 1, band] + got_y[lines - 1, band].astype(F32)
         for k in range(lines - 1):
-            piece += got_z[k, b * 8 : (b + 1) * 8].astype(F32)
+            piece += got_z[k, band].astype(F32)
         out[:, cut] = piece * cell_scaling(level[:, cut], label[:, cut], contrast, units)
-    for copy in c_copies[0] + c_copies[1] + y_copies + z_copies:
+    for copy in pending:
         copy.wait_send()
+    for k in range(lines):
+        twin_copy(0, k).wait_send()
+        twin_copy(1, k).wait_send()
+        y_copy(k).wait_send()
+        if k < lines - 1:
+            z_copy(k).wait_send()
 
 
 def params(number):
@@ -414,20 +479,37 @@
     parts = 4 if cell_blocks % 4 == 0 else 1
     dma = pltpu.SemaphoreType.DMA
 
+    capacity = max(2, 2 * tiles // peers)
+    size = min(GROUP, capacity)
+
     def own_part(table):
         return lax.dynamic_slice_in_dim(table.reshape(-1), own_index * tiles, tiles)
 
-    def places(owner, local, blocks, by_side):
-        owner, local = own_part(owner), own_part(local)
-        if by_side:
-            moved = (owner % 2 * 2 + owner // 2 % 2) * lines + owner // 4
-        else:
-            moved = owner % 2 * (peers // 2) + owner // 2
-        return owner * blocks + local, moved * blocks + local
-
-    col_take, col_put = places(col_owner, col_local, cell_blocks, True)
-    row_take, row_put = places(row_owner, row_local, station_blocks, False)
+    owner, local = own_part(col_owner), own_part(col_local)
+    row_who, row_where = own_part(row_owner), own_part(row_local)
     ranks = own_part(tile_rank)
+    col_take = owner * cell_blocks + local
+    row_take = row_who * station_blocks + row_where
+    row_put = (row_who % 2 * (peers // 2) + row_who // 2) * station_blocks + row_where
+
+    number = jnp.arange(tiles, dtype=jnp.int32)
+    earlier = (owner[None, :] == owner[:, None]) & (number[None, :] < number[:, None])
+    slot = owner * capacity + jnp.sum(earlier.astype(jnp.int32), axis=1)
+    rank_range = rank_max + 1
+    row_range = peers * station_blocks
+    packed = ((number * row_range + row_take) * rank_range + ranks) * cell_blocks + local
+    held = jnp.arange(peers * capacity, dtype=jnp.int32)[:, None] == slot[None, :]
+    packed = jnp.sum(jnp.where(held, packed[None, :], 0), axis=1)
+    slot_local = packed % cell_blocks
+    packed = packed // cell_blocks
+    slot_rank = packed % rank_range
+    packed = packed // rank_range
+    slot_row = packed % row_range
+    slot_tile = packed // row_range
+    target_row = (
+        slot_local[:, None] * 8 + jnp.arange(8, dtype=jnp.int32)[None, :]
+    ).reshape(peers * capacity // size, 1, size * 8)
+
     u_rows = u_factor.reshape(tiles * rank_max, width)
     v_rows = v_factor.reshape(tiles * rank_max, width)
     level = level_set.reshape(1, cell_total)
@@ -451,19 +533,31 @@
             peers * station_blocks, F32, rank_max,
         )
 
-    chunk = station_blocks * 8
+    small = station_blocks * 8
+    chunk = cell_blocks * 8
     pairs = peers // 2
-    with jax.named_scope("sum_stations"):
-        data = pl.pallas_call(
-            functools.partial(stations_kernel, pairs),
-            out_shape=jax.ShapeDtypeStruct((peers, station_blocks, 16, half), BF16),
-            in_specs=[VM, VM],
-            out_specs=ANY,
+    factors = pltpu.VMEM((tiles, rank_max, width), BF16)
+    with jax.named_scope("stations_and_adjoint"):
+        return pl.pallas_call(
+            functools.partial(adjoint_kernel, lines, units, capacity, rank_max),
+            out_shape=jax.ShapeDtypeStruct(probes.shape, F32),
+            in_specs=[SM, SM, SM, SM, VM, VM, VM, VM, VM, ANY, ANY],
+            out_specs=VM,
             scratch_shapes=[
-                pltpu.VMEM((pairs, chunk, width), F32),
-                pltpu.VMEM((pairs - 1, chunk, width), BF16),
-                pltpu.VMEM((pairs - 1, chunk, width), BF16),
+                factors,
+                factors,
+                pltpu.VMEM((peers * station_blocks, 16, half), BF16),
+                pltpu.VMEM((pairs, small, width), F32),
+                pltpu.VMEM((pairs - 1, small, width), BF16),
+                pltpu.VMEM((pairs - 1, small, width), BF16),
                 pltpu.VMEM((station_blocks, 16, half), BF16),
+                pltpu.VMEM((2, lines, chunk, width), BF16),
+                pltpu.VMEM((2, lines, chunk, width), BF16),
+                pltpu.VMEM((lines, chunk, width), BF16),
+                pltpu.VMEM((lines, chunk, width), BF16),
+                pltpu.VMEM((lines, chunk, width), F32),
+                pltpu.VMEM((lines - 1, chunk, width), BF16),
+                pltpu.VMEM((lines - 1, chunk, width), BF16),
                 dma((pairs,)),
                 dma((pairs,)),
                 dma((pairs - 1,)),
@@ -473,29 +567,8 @@
                 dma((pairs,)),
                 dma((pairs,)),
                 dma,
-            ],
-            compiler_params=params(1),
-        )(weight, partial)
-
-    with jax.named_scope("adjoint_tiles"):
-        spread = apply_tiles(
-            row_take, col_put, ranks, data.reshape(-1, 16, half), u_rows, v_rows,
-            peers * cell_blocks, BF16, rank_max,
-        )
-
-    chunk = cell_blocks * 8
-    with jax.named_scope("sum_cells"):
-        return pl.pallas_call(
-            functools.partial(back_kernel, lines, units),
-            out_shape=jax.ShapeDtypeStruct(probes.shape, F32),
-            in_specs=[SM, VM, VM, VM],
-            out_specs=VM,
-            scratch_shapes=[
-                pltpu.VMEM((2, lines, chunk, width), BF16),
-                pltpu.VMEM((lines, chunk, width), BF16),
-                pltpu.VMEM((lines, chunk, width), BF16),
-                pltpu.VMEM((lines - 1, chunk, width), BF16),
-                pltpu.VMEM((lines - 1, chunk, width), BF16),
+                dma,
+                dma,
                 dma((2, lines)),
                 dma((2, lines)),
                 dma((lines,)),
@@ -503,8 +576,11 @@
                 dma((lines - 1,)),
                 dma((lines - 1,)),
             ],
-            compiler_params=params(2),
-        )(contrast, level, label, spread)
+            compiler_params=params(1),
+        )(
+            contrast, slot_tile, slot_row, slot_rank, target_row, level, label, weight, partial,
+            u_factor, v_factor,
+        )
 
 
 def solution(mesh):

time: 93.3 us -> 84.3 us (0.904)
  Pallas kernels: 88.6 us -> 78 us
  other arithmetic: 1.38 us -> 4.09 us
  local copies, waits for them, and re-layouts: 2.93 us -> 1.98 us
    pallas_call x2 -> x1, Pallas kernels: 15.6 us -> 7.76 us  [apply_tiles(): pl.pallas_call(functools.partial(tiles_kernel, per_step, rank_max), out_s...]
    pallas_call x2 -> x1, Pallas kernels: 47.2 us -> 44.5 us  [shards(): pl.pallas_call(functools.partial(adjoint_kernel, lines, units, capacity,...]
    select_n x0 -> x3, other arithmetic: none -> 1.76 us  [the longest x1 0.6 us: shards(): slot_rank = packed % rank_range]
    dynamic_slice x1 -> x0, local copies, waits for them, and re-layouts: 1.26 us -> none  [own_part(): return lax.dynamic_slice_in_dim(table.reshape(-1), own_index * tiles, tiles)]
    add x1 -> x3, other arithmetic: 1.38 us -> 2.03 us  [the longest x1 1.39 us: shards(): ((number * row_range + row_take) * rank_range + ranks) * cell_blocks + local]
where the time goes in v2:
time: 84.3 us; the launch traced here: 84.1 us
  Pallas kernels  78 us (93%)
  other arithmetic  4.09 us (5%)
  local copies, waits for them, and re-layouts  1.98 us (2%)
    pallas_call x1, Pallas kernels, shards(): pl.pallas_call(functools.partial(adjoint_kernel, lines, units, capacity,...  44.5 us
    pallas_call x1, Pallas kernels, shards(): pl.pallas_call(functools.partial(cells_kernel, lines, units, parts), out_...  25.7 us
    pallas_call x1, Pallas kernels, apply_tiles(): pl.pallas_call(functools.partial(tiles_kernel, per_step, rank_max), out_s...  7.76 us

profile of v2, /device:TPU:0, one launch (start us, length us, event | category | flops | bytes accessed | tf_op | source)
XLA Modules:
  0.0 84.1 jit_solution(11020223405365912677)
XLA Ops:
  0.0 1.4 %multiply_add_fusion.1 = (s32[128]{0:T(128)S(1)}, s32[128]{0:T(128)}, s32[128]{0:T(128)}, s32[128]{0:T(128)}, s32[128]{0:T(128)S(1)}) fusion(s32[2048,1]{0,1:T(1,128)} %param.21, s32[]{:T(128)S(6)} %select_n.52, s32[2048]{0:T(1024)} %param.20, s32[2048]{0:T(1024)} %param.22, s32[2048]{0:T(1024)} %param.23, s32[2048,1]{0,1:T(1,128)} %param.19), kind=kLoop, calls=%fused_computation.37 | loop fusion | flops 4224 | bytes 5124 | tf_op jit(solution)/shard_map/add | solution.py:500
  1.4 0.2 convert_reduce_fusion
  1.6 0.1 select_reduce_fusion
  1.7 0.6 and_select_fusion.2
  2.3 0.6 and_select_fusion.3
  2.9 0.6 and_select_fusion.4.slot_tile
  3.5 0.1 add.101
  3.5 0.1 reduce_sum.22
  3.6 0.1 copy.17
  3.7 0.1 copy.20
  3.8 0.6 add.103.target_row
  4.4 25.7 %gather_cells.1 = bf16[16,16,16,256]{3,2,1,0:T(8,128)(2,1)} custom-call(f32[4]{0:T(128)} %contrast.3, f32[8,8192]{1,0:T(8,128)} %probes.1, f32[1,8192]{1,0:T(1,128)} %bitcast.38, s32[1,8192]{1,0:T(1,128)} %bitcast.40), custom_call_target="tpu_custom_call" | custom-call | tf_op jit(solution)/shard_map/gather_cells/pallas_call | solution.py:520
  30.2 7.8 %forward_tiles.1.part = f32[512,512]{1,0:T(8,128)} custom-call(s32[128]{0:T(128)} %get-tuple-element.14.take, s32[128]{0:T(128)} %get-tuple-element.13.put, s32[128]{0:T(128)} %get-tuple-element.12.ranks, bf16[256,16,256]{2,1,0:T(8,128)(2,1)} %bitcast.36, bf16[4096,512]{1,0:T(8,128)(2,1)} %bitcast.34, bf16[4096,512]{1,0:T(8,128)(2,1)} %bitcast.35), custom_call_target="tpu_custom_call" | custom-call | flops 536870912 | bytes 8388608 | tf_op jit(solution)/shard_map/forward_tiles/pallas_call | solution.py:206
  38.0 44.5 %stations_and_adjoint.1 = f32[8,8192]{1,0:T(8,128)} custom-call(f32[4]{0:T(128)} %contrast.3, s32[256]{0:T(256)} %and_select_fusion.4.slot_tile, s32[256]{0:T(256)} %get-tuple-element.9.slot_row, s32[256]{0:T(256)} %get-tuple-element.7.slot_rank, s32[32,1,64]{2,1,0:T(1,128)} %add.103.target_row, f32[1,8192]{1,0:T(1,128)} %bitcast.39, s32[1,8192]{1,0:T(1,128)} %bitcast.41, ...), custom_call_target="tpu_custom_call" | custom-call | tf_op jit(solution)/shard_map/stations_and_adjoint/pallas_call | solution.py:541
  82.4 1.7 %copy.23 = f32[8,8192]{1,0:T(8,128)} copy(f32[8,8192]{1,0:T(8,128)} %stations_and_adjoint.1) | data formatting | bytes 524288
  (5 shorter events, 0.0 us)

commit v3 on v2

v3 whole, which is shorter than its diff:
```python
import functools

import jax
import jax.numpy as jnp
from jax import lax
from jax.experimental import pallas as pl
from jax.experimental.pallas import tpu as pltpu
from jax.sharding import PartitionSpec as P

MESH = pl.DeviceIdType.MESH
VMEM_LIMIT = 56 * 1024 * 1024
GROUP = 8
F32 = jnp.float32
BF16 = jnp.bfloat16


def place(lines):
    me = lax.axis_index("tile")
    core = lax.rem(me, 2)
    side = lax.rem(me // 2, 2)
    step = me // 4
    return me, core, side, step


def index_of(step, side, core):
    return (step * 2 + side) * 2 + core


def remote(src, dst, send, recv, peer):
    return pltpu.make_async_remote_copy(
        src_ref=src,
        dst_ref=dst,
        send_sem=send,
        recv_sem=recv,
        device_id={"tile": peer},
        device_id_type=MESH,
    )


def gather_shards(lines, parts, fill, own, out, local_sem, sems, step, side, core):
    send_z, recv_z, send_y, recv_y, send_c, recv_c = sems
    me = index_of(step, side, core)
    across = index_of(step, 1 - side, core)
    twin = index_of(step, side, 1 - core)
    count = own.shape[0]
    size = count // parts
    started = []

    def at(slot, p):
        return out.at[pl.ds(slot * count + p * size, size)]

    def go(src, slot, p, send, recv, peer):
        copy = remote(src, at(slot, p), send, recv, peer)
        copy.start()
        started.append(copy)

    def arrived(slot, p, recv, peer):
        remote(at(slot, p), at(slot, p), recv, recv, peer).wait_recv()

    for p in range(parts):
        fill(p)
        piece = own.at[pl.ds(p * size, size)]
        go(piece, me, p, send_y.at[0, p], recv_y.at[0, p], across)
        for d in range(1, lines):
            peer = index_of(lax.rem(step + d, lines), side, core)
            go(piece, me, p, send_z.at[d - 1, p], recv_z.at[d - 1, p], peer)
    for p in range(parts):
        piece = own.at[pl.ds(p * size, size)]
        go(piece, me, p, send_c.at[0, p], recv_c.at[0, p], twin)
    mine = pltpu.make_async_copy(own, out.at[pl.ds(me * count, count)], local_sem)
    mine.start()

    for p in range(parts + 1):
        if p < parts:
            for k in range(1, lines):
                slot = index_of(lax.rem(step + lines - k, lines), side, core)
                arrived(slot, p, recv_z.at[k - 1, p], me)
                go(at(slot, p), slot, p, send_y.at[k, p], recv_y.at[k, p], across)
                go(at(slot, p), slot, p, send_c.at[k, p], recv_c.at[k, p], twin)
        if p >= 1:
            for k in range(lines):
                slot = index_of(lax.rem(step + lines - k, lines), 1 - side, core)
                arrived(slot, p - 1, recv_y.at[k, p - 1], across)
                far = lines + k
                go(
                    at(slot, p - 1), slot, p - 1,
                    send_c.at[far, p - 1], recv_c.at[far, p - 1], twin,
                )
    for p in range(parts):
        for k in range(lines):
            for far in range(2):
                where = 1 - side if far else side
                slot = index_of(lax.rem(step + lines - k, lines), where, 1 - core)
                arrived(slot, p, recv_c.at[far * lines + k, p], twin)
    mine.wait()
    return started


def gather_sems(lines, parts):
    dma = pltpu.SemaphoreType.DMA
    return [
        dma((lines - 1, parts)),
        dma((lines - 1, parts)),
        dma((lines, parts)),
        dma((lines, parts)),
        dma((2 * lines, parts)),
        dma((2 * lines, parts)),
    ]


def cell_scaling(level, label, contrast, units):
    picked = jnp.full(level.shape, contrast[0], F32)
    for unit in range(1, units):
        picked = jnp.where(label == unit, contrast[unit], picked)
    return picked / (1.0 + level * level)


def halves(block):
    half = block.shape[1] // 2
    return jnp.concatenate([block[:, :half], block[:, half:]], axis=0)


def block_chunks(owners, tables, capacity, rank_max, chunk, source, inward, outward):
    tile_of, block_of, rank_of, target_row = tables
    size = min(GROUP, capacity)
    groups = capacity // size
    rows = size * rank_max
    lane = lax.broadcasted_iota(jnp.int32, (8, rows), 1)
    line = lax.broadcasted_iota(jnp.int32, (chunk, size * 8), 0)
    jobs = [(o, g) for o in owners for g in range(groups)]
    inners = []
    for o, g in jobs:
        pieces, factors = [], []
        for j in range(size):
            s = o * capacity + g * size + j
            block = source[block_of[s]].astype(F32)
            pieces.append(jnp.concatenate([block[:8], block[8:]], axis=1))
            factors.append(inward[tile_of[s]])
        inners.append(
            lax.dot_general(
                jnp.concatenate(pieces, axis=0).astype(BF16),
                jnp.concatenate(factors, axis=0),
                (((1,), (1,)), ((), ())),
                preferred_element_type=F32,
            )
        )
    spread = []
    for (o, g), inner in zip(jobs, inners):
        kept = []
        for j in range(size):
            start = j * rank_max
            end = start + rank_of[o * capacity + g * size + j]
            piece = inner[j * 8 : (j + 1) * 8]
            kept.append(jnp.where((lane >= start) & (lane < end), piece, 0.0))
        kept = jnp.concatenate(kept, axis=0).astype(BF16)
        chosen = jnp.where(line == target_row[o * groups + g], 1.0, 0.0).astype(BF16)
        spread.append(jnp.dot(chosen, kept, preferred_element_type=F32).astype(BF16))
    values = []
    for n in range(len(owners)):
        value = None
        for g in range(groups):
            s = owners[n] * capacity + g * size
            factors = jnp.concatenate([outward[tile_of[s + j]] for j in range(size)], axis=0)
            term = jnp.dot(spread[n * groups + g], factors, preferred_element_type=F32)
            value = term if value is None else value + term
        values.append(value)
    return values


def stations_phase(
    pairs, chunks, weight, out,
    part, near, got_c, send_line, got_line, own,
    c_send, c_recv, l_send, l_recv, a_send, a_recv, t_send, t_recv, local_sem
):
    me = lax.axis_index("tile")
    core = lax.rem(me, 2)
    pair = me // 2
    twin = pair * 2 + 1 - core
    count = own.shape[0]
    width = part.shape[2]

    def peer(d):
        return lax.rem(pair + d, pairs) * 2 + core

    def shard(slot):
        return out.at[pl.ds(slot * count, count)]

    def c_copy(i):
        return remote(part.at[i], got_c.at[i], c_send.at[i], c_recv.at[i], twin)

    def line(i):
        return remote(
            send_line.at[i], got_line.at[i], l_send.at[i], l_recv.at[i], peer(i + 1)
        )

    def one_pair(i, _):
        there = lax.rem(pair + i + 1, pairs) * 2
        first, second = chunks([there + 1 - core, there + core])
        part[i] = first
        c_copy(i).start()
        near[i] = second

        @pl.when(i > 0)
        def _():
            c_copy(i - 1).wait_recv()
            send_line[i - 1] = (near[i - 1] + got_c[i - 1]).astype(BF16)
            line(i - 1).start()

        return 0

    lax.fori_loop(0, pairs, one_pair, 0)
    c_copy(pairs - 1).wait_recv()
    total = near[pairs - 1] + got_c[pairs - 1]
    copies = [c_copy(i) for i in range(pairs)]
    lines = [line(i) for i in range(pairs - 1)]
    for i in range(pairs - 1):
        lines[i].wait_recv()
        total += got_line[i].astype(F32)
    for b in range(count):
        start = pl.multiple_of(me * (count * width) + b * width, width)
        factor = weight[:, pl.ds(start, width)]
        own[b] = halves(total[b * 8 : (b + 1) * 8] * factor).astype(BF16)
    sent = []

    def go(src, slot, send, recv, target):
        copy = remote(src, shard(slot), send, recv, target)
        copy.start()
        sent.append(copy)

    for d in range(1, pairs):
        go(own, me, a_send.at[d - 1], a_recv.at[d - 1], peer(d))
    go(own, me, t_send.at[0], t_recv.at[0], twin)
    mine = pltpu.make_async_copy(own, shard(me), local_sem)
    mine.start()
    for d in range(1, pairs):
        slot = peer(pairs - d)
        remote(own, shard(slot), a_send.at[d - 1], a_recv.at[d - 1], slot).wait_recv()
        go(shard(slot), slot, t_send.at[d], t_recv.at[d], twin)
    for d in range(pairs):
        slot = lax.rem(pair + pairs - d, pairs) * 2 + 1 - core
        remote(own, shard(slot), t_send.at[d], t_recv.at[d], twin).wait_recv()
    mine.wait()
    return copies + lines + sent


def whole_kernel(
    lines, units, parts, capacity, rank_max,
    contrast, row_tile, row_block, row_rank, col_tile, col_block, col_rank,
    row_target, col_target, probes, level, label, weight, u_hbm, v_hbm,
    out,
    u_here, v_here, cells, own_cells, data,
    part, near_part, got_c, send_line, got_line, own,
    send_twin, got_twin, send_y, got_y, near, send_z, got_z,
    c_send, c_recv, l_send, l_recv, a_send, a_recv, t_send, t_recv, local_sem, u_sem, v_sem,
    x_send, x_recv, y_send, y_recv, z_send, z_recv, cells_sem, *gather
):
    me, core, side, step = place(lines)
    pairs = 2 * lines
    across = index_of(step, 1 - side, core)
    twin = index_of(step, side, 1 - core)
    barrier = pltpu.get_barrier_semaphore()
    for d in range(1, pairs):
        peer = lax.rem(me // 2 + d, pairs) * 2 + core
        pl.semaphore_signal(barrier, inc=1, device_id={"tile": peer}, device_id_type=MESH)
    pl.semaphore_signal(barrier, inc=1, device_id={"tile": twin}, device_id_type=MESH)
    u_copy = pltpu.make_async_copy(u_hbm, u_here, u_sem)
    v_copy = pltpu.make_async_copy(v_hbm, v_here, v_sem)
    u_copy.start()
    v_copy.start()
    cell_count = own_cells.shape[0]
    width = probes.shape[1] // cell_count
    size = cell_count // parts

    def fill(p):
        for b in range(p * size, (p + 1) * size):
            cut = pl.ds(b * width, width)
            scaling = cell_scaling(level[:, cut], label[:, cut], contrast, units)
            own_cells[b] = halves(probes[:, cut] * scaling).astype(BF16)

    pl.semaphore_wait(barrier, pairs)
    pending = gather_shards(
        lines, parts, fill, own_cells, cells, cells_sem, gather, step, side, core
    )
    u_copy.wait()
    v_copy.wait()

    def station_chunks(owners):
        tables = (row_tile, row_block, row_rank, row_target)
        return block_chunks(
            owners, tables, capacity, rank_max, part.shape[1], cells, v_here, u_here
        )

    pending += stations_phase(
        pairs, station_chunks, weight, data,
        part, near_part, got_c, send_line, got_line, own,
        c_send, c_recv, l_send, l_recv, a_send, a_recv, t_send, t_recv, local_sem,
    )
    chunk = near.shape[1]

    def chunks(owners):
        tables = (col_tile, col_block, col_rank, col_target)
        return block_chunks(owners, tables, capacity, rank_max, chunk, data, u_here, v_here)

    def target(k):
        return lax.rem(step + k + 1, lines)

    def twin_copy(far, k):
        return remote(
            send_twin.at[far, k], got_twin.at[far, k], x_send.at[far, k], x_recv.at[far, k], twin
        )

    def y_copy(k):
        return remote(send_y.at[k], got_y.at[k], y_send.at[k], y_recv.at[k], across)

    def z_copy(k):
        return remote(
            send_z.at[k], got_z.at[k], z_send.at[k], z_recv.at[k],
            index_of(target(k), side, core),
        )

    def one_target(k, _):
        there = target(k)
        first, second = chunks(
            [index_of(there, 1 - side, 1 - core), index_of(there, side, 1 - core)]
        )
        send_twin[0, k] = first.astype(BF16)
        twin_copy(0, k).start()
        send_twin[1, k] = second.astype(BF16)
        twin_copy(1, k).start()
        first, second = chunks([index_of(there, 1 - side, core), index_of(there, side, core)])
        twin_copy(0, k).wait_recv()
        send_y[k] = (first + got_twin[0, k].astype(F32)).astype(BF16)
        y_copy(k).start()
        twin_copy(1, k).wait_recv()
        near[k] = second + got_twin[1, k].astype(F32)

        @pl.when(k > 0)
        def _():
            y_copy(k - 1).wait_recv()
            send_z[k - 1] = (near[k - 1] + got_y[k - 1].astype(F32)).astype(BF16)
            z_copy(k - 1).start()

        return 0

    lax.fori_loop(0, lines, one_target, 0)
    y_copy(lines - 1).wait_recv()
    for k in range(lines - 1):
        z_copy(k).wait_recv()
    for b in range(chunk // 8):
        cut = pl.ds(b * width, width)
        band = slice(b * 8, (b + 1) * 8)
        piece = near[lines - 1, band] + got_y[lines - 1, band].astype(F32)
        for k in range(lines - 1):
            piece += got_z[k, band].astype(F32)
        out[:, cut] = piece * cell_scaling(level[:, cut], label[:, cut], contrast, units)
    for copy in pending:
        copy.wait_send()
    for k in range(lines):
        twin_copy(0, k).wait_send()
        twin_copy(1, k).wait_send()
        y_copy(k).wait_send()
        if k < lines - 1:
            z_copy(k).wait_send()


def params(number):
    return pltpu.CompilerParams(
        collective_id=number, has_side_effects=True, vmem_limit_bytes=VMEM_LIMIT
    )


VM = pl.BlockSpec(memory_space=pltpu.VMEM)
SM = pl.BlockSpec(memory_space=pltpu.SMEM)
ANY = pl.BlockSpec(memory_space=pl.ANY)


def shards(
    probes,
    level_set,
    unit_label,
    contrast,
    station_weight,
    u_factor,
    v_factor,
    col_owner,
    col_local,
    row_owner,
    row_local,
    tile_rank,
):
    peers = lax.axis_size("tile")
    lines = peers // 4
    own_index = lax.axis_index("tile")
    tiles, rank_max, width = u_factor.shape
    cell_total = probes.shape[1]
    cell_blocks = cell_total // width
    station_blocks = station_weight.shape[0] // (peers * width)
    units = contrast.shape[0]
    half = width // 2
    parts = 4 if cell_blocks % 4 == 0 else 1
    dma = pltpu.SemaphoreType.DMA

    capacity = max(2, 2 * tiles // peers)
    size = min(GROUP, capacity)

    def own_part(table):
        return lax.dynamic_slice_in_dim(table.reshape(-1), own_index * tiles, tiles)

    owner, local = own_part(col_owner), own_part(col_local)
    row_who, row_where = own_part(row_owner), own_part(row_local)
    ranks = own_part(tile_rank)
    col_take = owner * cell_blocks + local
    row_take = row_who * station_blocks + row_where

    number = jnp.arange(tiles, dtype=jnp.int32)
    rank_range = rank_max + 1

    def slots(owner, local, local_range, block, block_range):
        earlier = (owner[None, :] == owner[:, None]) & (number[None, :] < number[:, None])
        slot = owner * capacity + jnp.sum(earlier.astype(jnp.int32), axis=1)
        packed = ((number * block_range + block) * rank_range + ranks) * local_range + local
        held = jnp.arange(peers * capacity, dtype=jnp.int32)[:, None] == slot[None, :]
        packed = jnp.sum(jnp.where(held, packed[None, :], 0), axis=1)
        where = packed % local_range
        packed = packed // local_range
        rank = packed % rank_range
        packed = packed // rank_range
        target = where[:, None] * 8 + jnp.arange(8, dtype=jnp.int32)[None, :]
        target = target.reshape(peers * capacity // size, 1, size * 8)
        return packed // block_range, packed % block_range, rank, target

    row_tile, row_block, row_rank, row_target = slots(
        row_who, row_where, station_blocks, col_take, peers * cell_blocks
    )
    col_tile, col_block, col_rank, col_target = slots(
        owner, local, cell_blocks, row_take, peers * station_blocks
    )
    level = level_set.reshape(1, cell_total)
    label = unit_label.reshape(1, cell_total)
    weight = station_weight.reshape(1, -1)

    small = station_blocks * 8
    chunk = cell_blocks * 8
    pairs = peers // 2
    factors = pltpu.VMEM((tiles, rank_max, width), BF16)
    with jax.named_scope("hessian_kernel"):
        return pl.pallas_call(
            functools.partial(whole_kernel, lines, units, parts, capacity, rank_max),
            out_shape=jax.ShapeDtypeStruct(probes.shape, F32),
            in_specs=[SM] * 7 + [VM] * 6 + [ANY] * 2,
            out_specs=VM,
            scratch_shapes=[
                factors,
                factors,
                pltpu.VMEM((peers * cell_blocks, 16, half), BF16),
                pltpu.VMEM((cell_blocks, 16, half), BF16),
                pltpu.VMEM((peers * station_blocks, 16, half), BF16),
                pltpu.VMEM((pairs, small, width), F32),
                pltpu.VMEM((pairs, small, width), F32),
                pltpu.VMEM((pairs, small, width), F32),
                pltpu.VMEM((pairs - 1, small, width), BF16),
                pltpu.VMEM((pairs - 1, small, width), BF16),
                pltpu.VMEM((station_blocks, 16, half), BF16),
                pltpu.VMEM((2, lines, chunk, width), BF16),
                pltpu.VMEM((2, lines, chunk, width), BF16),
                pltpu.VMEM((lines, chunk, width), BF16),
                pltpu.VMEM((lines, chunk, width), BF16),
                pltpu.VMEM((lines, chunk, width), F32),
                pltpu.VMEM((lines - 1, chunk, width), BF16),
                pltpu.VMEM((lines - 1, chunk, width), BF16),
                dma((pairs,)),
                dma((pairs,)),
                dma((pairs - 1,)),
                dma((pairs - 1,)),
                dma((pairs - 1,)),
                dma((pairs - 1,)),
                dma((pairs,)),
                dma((pairs,)),
                dma,
                dma,
                dma,
                dma((2, lines)),
                dma((2, lines)),
                dma((lines,)),
                dma((lines,)),
                dma((lines - 1,)),
                dma((lines - 1,)),
                dma,
            ]
            + gather_sems(lines, parts),
            compiler_params=params(0),
        )(
            contrast, row_tile, row_block, row_rank, col_tile, col_block, col_rank,
            row_target, col_target, probes, level, label, weight, u_factor, v_factor,
        )


def solution(mesh):
    placed = (
        P(None, ("groups", "tile")),
        P(("groups", "tile")),
        P(("groups", "tile")),
        P("groups"),
        P("groups"),
        P(("groups", "tile"), None, None),
        P(("groups", "tile"), None, None),
        P("groups", None),
        P("groups"),
        P("groups", None),
        P("groups"),
        P("groups"),
    )
    return jax.shard_map(
        shards, mesh=mesh, in_specs=placed, out_specs=P(None, ("groups", "tile")), check_vma=False
    )
```

time: 84.3 us -> 76 us (0.902)
  Pallas kernels: 78 us -> 68 us
  other arithmetic: 4.09 us -> 5.53 us
    pallas_call x3 -> x1, Pallas kernels: 78 us -> 68 us  [shards(): pl.pallas_call(functools.partial(whole_kernel, lines, units, parts, capac...]
    select_n x3 -> x6, other arithmetic: 1.76 us -> 3.55 us  [the longest x4 2.34 us: slots(): return (packed // block_range, packed % block_range, rank, target)]
    add x3 -> x4, other arithmetic: 2.03 us -> 1.46 us  [the longest x1 0.82 us: slots(): ((number * block_range + block) * rank_range + ranks) * local_range + local]
where the time goes in v3:
time: 76 us; the launch traced here: 75.8 us
  Pallas kernels  68 us (89%)
  other arithmetic  5.53 us (7%)
  local copies, waits for them, and re-layouts  2.22 us (3%)
    pallas_call x1, Pallas kernels, shards(): pl.pallas_call(functools.partial(whole_kernel, lines, units, parts, capac...  68 us
    select_n x4, other arithmetic, slots(): return (packed // block_range, packed % block_range, rank, target)  2.34 us
    unnamed x1, local copies, waits for them, and re-layouts  1.67 us

profile of v3, /device:TPU:0, one launch (start us, length us, event | category | flops | bytes accessed | tf_op | source)
XLA Modules:
  0.0 75.8 jit_solution(12751965929242672645)
XLA Ops:
  0.0 0.8 %multiply_add_fusion = (s32[128]{0:T(128)S(1)}, s32[128]{0:T(128)S(1)}, s32[128]{0:T(128)S(1)}, s32[128]{0:T(128)S(1)}) fusion(s32[2048]{0:T(1024)} %param.22, s32[]{:T(128)S(6)} %select_n.69, s32[2048]{0:T(1024)} %param.23, s32[2048]{0:T(1024)} %param.20, s32[2048,1]{0,1:T(1,128)} %param.21, s32[2048,1]{0,1:T(1,128)} %param.19), kind=kLoop, calls=%fused_computation.45 | loop fusion | flops 2048 | bytes 4612 | tf_op jit(solution)/shard_map/add | solution.py:421
  0.8 0.2 convert_reduce_fusion.1
  1.0 0.2 convert_reduce_fusion
  1.2 0.2 select_reduce_fusion
  1.4 0.6 and_select_fusion
  2.0 0.6 and_select_fusion.1
  2.6 0.5 and_select_fusion.2.col_tile
  3.1 0.6 and_select_fusion.5
  3.7 0.6 and_select_fusion.6
  4.3 0.6 and_select_fusion.7.row_tile
  4.9 0.1 add.156
  5.0 0.1 reduce_sum.44
  5.1 0.1 copy.21
  5.2 0.1 reduce_sum.45
  5.2 0.1 copy.26
  5.4 0.1 copy.29
  5.4 0.1 copy.24
  5.5 0.6 fusion.6
  6.1 68.0 %hessian_kernel.1 = f32[8,8192]{1,0:T(8,128)} custom-call(f32[4]{0:T(128)} %contrast.1, s32[256]{0:T(256)} %and_select_fusion.7.row_tile, s32[256]{0:T(256)} %get-tuple-element.13.row_block, s32[256]{0:T(256)} %get-tuple-element.11.row_rank, s32[256]{0:T(256)} %and_select_fusion.2.col_tile, s32[256]{0:T(256)} %get-tuple-element.7.col_block, ...), custom_call_target="tpu_custom_call" | custom-call | tf_op jit(solution)/shard_map/hessian_kernel/pallas_call | solution.py:447
  74.2 1.7 %copy.32 = f32[8,8192]{1,0:T(8,128)} copy(f32[8,8192]{1,0:T(8,128)} %hessian_kernel.1) | data formatting | bytes 524288
  (8 shorter events, 0.1 us)

commit v4 on v3

--- a/solution.py
+++ b/solution.py
@@ -120,22 +120,26 @@
     return jnp.concatenate([block[:, :half], block[:, half:]], axis=0)
 
 
+def bits_of(limit):
+    return max(1, (limit - 1).bit_length())
+
+
 def block_chunks(owners, tables, capacity, rank_max, chunk, source, inward, outward):
-    tile_of, block_of, rank_of, target_row = tables
+    codes, lane_block, shift, tile_shift = tables
+    block_mask = (1 << (tile_shift - shift)) - 1
     size = min(GROUP, capacity)
     groups = capacity // size
     rows = size * rank_max
     lane = lax.broadcasted_iota(jnp.int32, (8, rows), 1)
-    line = lax.broadcasted_iota(jnp.int32, (chunk, size * 8), 0)
     jobs = [(o, g) for o in owners for g in range(groups)]
     inners = []
     for o, g in jobs:
         pieces, factors = [], []
         for j in range(size):
-            s = o * capacity + g * size + j
-            block = source[block_of[s]].astype(F32)
+            code = codes[o * capacity + g * size + j]
+            block = source[(code >> shift) & block_mask].astype(F32)
             pieces.append(jnp.concatenate([block[:8], block[8:]], axis=1))
-            factors.append(inward[tile_of[s]])
+            factors.append(inward[code >> tile_shift])
         inners.append(
             lax.dot_general(
                 jnp.concatenate(pieces, axis=0).astype(BF16),
@@ -146,21 +150,23 @@
         )
     spread = []
     for (o, g), inner in zip(jobs, inners):
-        kept = []
-        for j in range(size):
-            start = j * rank_max
-            end = start + rank_of[o * capacity + g * size + j]
-            piece = inner[j * 8 : (j + 1) * 8]
-            kept.append(jnp.where((lane >= start) & (lane < end), piece, 0.0))
-        kept = jnp.concatenate(kept, axis=0).astype(BF16)
-        chosen = jnp.where(line == target_row[o * groups + g], 1.0, 0.0).astype(BF16)
-        spread.append(jnp.dot(chosen, kept, preferred_element_type=F32).astype(BF16))
+        compact = inner[:8]
+        for j in range(1, size):
+            compact = jnp.where(lane >= j * rank_max, inner[j * 8 : (j + 1) * 8], compact)
+        where = jnp.broadcast_to(lane_block[o * groups + g], (8, rows))
+        spread.append(
+            jnp.concatenate(
+                [jnp.where(where == b, compact, 0.0) for b in range(chunk // 8)], axis=0
+            ).astype(BF16)
+        )
     values = []
     for n in range(len(owners)):
         value = None
         for g in range(groups):
             s = owners[n] * capacity + g * size
-            factors = jnp.concatenate([outward[tile_of[s + j]] for j in range(size)], axis=0)
+            factors = jnp.concatenate(
+                [outward[codes[s + j] >> tile_shift] for j in range(size)], axis=0
+            )
             term = jnp.dot(spread[n * groups + g], factors, preferred_element_type=F32)
             value = term if value is None else value + term
         values.append(value)
@@ -244,9 +250,8 @@
 
 
 def whole_kernel(
-    lines, units, parts, capacity, rank_max,
-    contrast, row_tile, row_block, row_rank, col_tile, col_block, col_rank,
-    row_target, col_target, probes, level, label, weight, u_hbm, v_hbm,
+    lines, units, parts, capacity, rank_max, row_shifts, col_shifts,
+    contrast, row_codes, col_codes, row_lanes, col_lanes, probes, level, label, weight, u_hbm, v_hbm,
     out,
     u_here, v_here, cells, own_cells, data,
     part, near_part, got_c, send_line, got_line, own,
@@ -285,7 +290,7 @@
     v_copy.wait()
 
     def station_chunks(owners):
-        tables = (row_tile, row_block, row_rank, row_target)
+        tables = (row_codes, row_lanes) + row_shifts
         return block_chunks(
             owners, tables, capacity, rank_max, part.shape[1], cells, v_here, u_here
         )
@@ -298,7 +303,7 @@
     chunk = near.shape[1]
 
     def chunks(owners):
-        tables = (col_tile, col_block, col_rank, col_target)
+        tables = (col_codes, col_lanes) + col_shifts
         return block_chunks(owners, tables, capacity, rank_max, chunk, data, u_here, v_here)
 
     def target(k):
@@ -413,26 +418,27 @@
     row_take = row_who * station_blocks + row_where
 
     number = jnp.arange(tiles, dtype=jnp.int32)
-    rank_range = rank_max + 1
+    rank_bits = bits_of(rank_max + 1)
 
     def slots(owner, local, local_range, block, block_range):
+        shift = rank_bits + bits_of(local_range)
+        tile_shift = shift + bits_of(block_range)
         earlier = (owner[None, :] == owner[:, None]) & (number[None, :] < number[:, None])
         slot = owner * capacity + jnp.sum(earlier.astype(jnp.int32), axis=1)
-        packed = ((number * block_range + block) * rank_range + ranks) * local_range + local
+        code = (number << tile_shift) | (block << shift) | (local << rank_bits) | ranks
         held = jnp.arange(peers * capacity, dtype=jnp.int32)[:, None] == slot[None, :]
-        packed = jnp.sum(jnp.where(held, packed[None, :], 0), axis=1)
-        where = packed % local_range
-        packed = packed // local_range
-        rank = packed % rank_range
-        packed = packed // rank_range
-        target = where[:, None] * 8 + jnp.arange(8, dtype=jnp.int32)[None, :]
-        target = target.reshape(peers * capacity // size, 1, size * 8)
-        return packed // block_range, packed % block_range, rank, target
-
-    row_tile, row_block, row_rank, row_target = slots(
+        code = jnp.sum(jnp.where(held, code[None, :], 0), axis=1)
+        rank = code & ((1 << rank_bits) - 1)
+        where = (code >> rank_bits) & ((1 << (shift - rank_bits)) - 1)
+        kept = jnp.arange(rank_max, dtype=jnp.int32)[None, :] < rank[:, None]
+        lanes = jnp.where(kept, where[:, None], -1)
+        lanes = lanes.reshape(peers * capacity // size, 1, size * rank_max)
+        return code, lanes, (shift, tile_shift)
+
+    row_codes, row_lanes, row_shifts = slots(
         row_who, row_where, station_blocks, col_take, peers * cell_blocks
     )
-    col_tile, col_block, col_rank, col_target = slots(
+    col_codes, col_lanes, col_shifts = slots(
         owner, local, cell_blocks, row_take, peers * station_blocks
     )
     level = level_set.reshape(1, cell_total)
@@ -445,9 +451,11 @@
     factors = pltpu.VMEM((tiles, rank_max, width), BF16)
     with jax.named_scope("hessian_kernel"):
         return pl.pallas_call(
-            functools.partial(whole_kernel, lines, units, parts, capacity, rank_max),
+            functools.partial(
+                whole_kernel, lines, units, parts, capacity, rank_max, row_shifts, col_shifts
+            ),
             out_shape=jax.ShapeDtypeStruct(probes.shape, F32),
-            in_specs=[SM] * 7 + [VM] * 6 + [ANY] * 2,
+            in_specs=[SM] * 3 + [VM] * 6 + [ANY] * 2,
             out_specs=VM,
             scratch_shapes=[
                 factors,
@@ -490,8 +498,7 @@
             + gather_sems(lines, parts),
             compiler_params=params(0),
         )(
-            contrast, row_tile, row_block, row_rank, col_tile, col_block, col_rank,
-            row_target, col_target, probes, level, label, weight, u_factor, v_factor,
+            contrast, row_codes, col_codes, row_lanes, col_lanes, probes, level, label, weight, u_factor, v_factor,
         )
 
 

time: 76 us -> 72.4 us (0.953)
  other arithmetic: 5.53 us -> 2.04 us
  Pallas kernels: 68 us -> 67.1 us
    select_n x6 -> x1, other arithmetic: 3.55 us -> 0.7 us  [slots(): lanes = jnp.where(kept, where[:, None], -1)]
    add x2 -> x0, other arithmetic: 1.45 us -> none  [the longest x1 0.82 us: slots(): ((number * block_range + block) * rank_range + ranks) * local_range + local]
    pallas_call x1, Pallas kernels: 68 us -> 67.1 us  [shards(): pl.pallas_call(functools.partial(whole_kernel, lines, units, parts, capac...]
    or x0 -> x1, other arithmetic: none -> 0.82 us  [slots(): code = number << tile_shift | block << shift | local << rank_bits | ranks]
    unnamed x1 -> x5, local copies, waits for them, and re-layouts: 1.67 us -> 1.68 us
where the time goes in v4:
time: 72.4 us; the launch traced here: 72.2 us
  Pallas kernels  67.1 us (93%)
  local copies, waits for them, and re-layouts  2.95 us (4%)
  other arithmetic  2.04 us (3%)
    pallas_call x1, Pallas kernels, shards(): pl.pallas_call(functools.partial(whole_kernel, lines, units, parts, capac...  67.1 us
    unnamed x5, local copies, waits for them, and re-layouts  1.68 us

profile of v4, /device:TPU:0, one launch (start us, length us, event | category | flops | bytes accessed | tf_op | source)
XLA Modules:
  0.0 72.2 jit_solution(9223380629896336958)
XLA Ops:
  0.0 0.8 %or_or_fusion = (s32[128]{0:T(128)S(1)}, s32[128]{0:T(128)S(1)}, s32[128]{0:T(128)S(1)}, s32[128]{0:T(128)S(1)}) fusion(s32[2048]{0:T(1024)} %param.23, s32[]{:T(128)S(6)} %select_n.35, s32[2048]{0:T(1024)} %param.22, s32[2048]{0:T(1024)} %param.20, s32[2048,1]{0,1:T(1,128)} %param.21, s32[2048,1]{0,1:T(1,128)} %param.19), kind=kLoop, calls=%fused_computation.15 | loop fusion | flops 1920 | bytes 4612 | tf_op jit(solution)/shard_map/or | solution.py:428
  0.8 0.2 convert_reduce_fusion.1
  1.0 0.2 convert_reduce_fusion
  1.2 0.2 select_reduce_fusion
  1.4 0.0 copy-start
  1.4 0.0 copy-start.1
  1.4 0.1 lt.90
  1.5 0.1 and.56
  1.6 0.1 and.61
  1.6 0.1 and.59
  1.7 0.1 and.64
  1.8 0.1 broadcast_in_dim.66
  1.9 0.1 broadcast_in_dim.67
  2.1 0.1 broadcast_in_dim.63
  2.2 0.1 broadcast_in_dim.64
  2.3 0.1 lt.95
  2.4 0.1 lt.96
  2.5 0.1 lt.92
  2.6 0.1 lt.93
  2.7 0.7 compare_select_fusion
  3.5 0.0 copy-done
  3.5 0.0 copy-done.1
  3.5 67.1 %hessian_kernel.1 = f32[8,8192]{1,0:T(8,128)} custom-call(f32[4]{0:T(128)} %contrast.1, s32[256]{0:T(256)} %copy-done.1, s32[256]{0:T(256)} %copy-done, s32[32,1,256]{2,1,0:T(1,128)} %get-tuple-element.12.row_lanes, s32[32,1,256]{2,1,0:T(1,128)} %get-tuple-element.11.col_lanes, f32[8,8192]{1,0:T(8,128)} %probes.1, f32[1,8192]{1,0:T(1,128)} %bitcast.10, ...), custom_call_target="tpu_custom_call" | custom-call | tf_op jit(solution)/shard_map/hessian_kernel/pallas_call | solution.py:453
  70.6 1.7 %copy.14 = f32[8,8192]{1,0:T(8,128)} copy(f32[8,8192]{1,0:T(8,128)} %hessian_kernel.1) | data formatting | bytes 524288
  (5 shorter events, 0.0 us)
Async XLA Ops:
  1.4 2.1 %copy-start = (s32[256]{0:T(256)}, s32[256]{0:T(256)S(1)}, u32[]{:S(2)}) copy-start(s32[256]{0:T(256)S(1)} %get-tuple-element.17.col_codes) | copy-start | bytes 3076
  1.4 2.1 %copy-start.1 = (s32[256]{0:T(256)}, s32[256]{0:T(256)S(1)}, u32[]{:S(2)}) copy-start(s32[256]{0:T(256)S(1)} %get-tuple-element.18.row_codes) | copy-start | bytes 3076

commit v5 on v4

--- a/solution.py
+++ b/solution.py
@@ -20,6 +20,15 @@
     side = lax.rem(me // 2, 2)
     step = me // 4
     return me, core, side, step
+
+
+def crossed(step, turn, lines):
+    result, weight = 0, 1
+    while weight < lines:
+        one, two = lax.rem(step // weight, 2), (turn // weight) % 2
+        result += (one + two - 2 * one * two) * weight
+        weight *= 2
+    return result
 
 
 def index_of(step, side, core):
@@ -61,8 +70,8 @@
         fill(p)
         piece = own.at[pl.ds(p * size, size)]
         go(piece, me, p, send_y.at[0, p], recv_y.at[0, p], across)
-        for d in range(1, lines):
-            peer = index_of(lax.rem(step + d, lines), side, core)
+        for d in reversed(range(1, lines)):
+            peer = index_of(crossed(step, d, lines), side, core)
             go(piece, me, p, send_z.at[d - 1, p], recv_z.at[d - 1, p], peer)
     for p in range(parts):
         piece = own.at[pl.ds(p * size, size)]
@@ -73,13 +82,13 @@
     for p in range(parts + 1):
         if p < parts:
             for k in range(1, lines):
-                slot = index_of(lax.rem(step + lines - k, lines), side, core)
+                slot = index_of(crossed(step, k, lines), side, core)
                 arrived(slot, p, recv_z.at[k - 1, p], me)
                 go(at(slot, p), slot, p, send_y.at[k, p], recv_y.at[k, p], across)
                 go(at(slot, p), slot, p, send_c.at[k, p], recv_c.at[k, p], twin)
         if p >= 1:
             for k in range(lines):
-                slot = index_of(lax.rem(step + lines - k, lines), 1 - side, core)
+                slot = index_of(crossed(step, k, lines), 1 - side, core)
                 arrived(slot, p - 1, recv_y.at[k, p - 1], across)
                 far = lines + k
                 go(
@@ -90,7 +99,7 @@
         for k in range(lines):
             for far in range(2):
                 where = 1 - side if far else side
-                slot = index_of(lax.rem(step + lines - k, lines), where, 1 - core)
+                slot = index_of(crossed(step, k, lines), where, 1 - core)
                 arrived(slot, p, recv_c.at[far * lines + k, p], twin)
     mine.wait()
     return started
@@ -307,7 +316,7 @@
         return block_chunks(owners, tables, capacity, rank_max, chunk, data, u_here, v_here)
 
     def target(k):
-        return lax.rem(step + k + 1, lines)
+        return crossed(step, lines - 1 - k, lines)
 
     def twin_copy(far, k):
         return remote(

time: 72.4 us -> 72.8 us (level)
  no operation moved by 1% of the time
where the time goes in v5:
time: 72.8 us; the launch traced here: 72.6 us
  Pallas kernels  67.4 us (93%)
  local copies, waits for them, and re-layouts  2.95 us (4%)
  other arithmetic  2.04 us (3%)
    pallas_call x1, Pallas kernels, shards(): pl.pallas_call(functools.partial(whole_kernel, lines, units, parts, capac...  67.4 us
    unnamed x5, local copies, waits for them, and re-layouts  1.68 us

profile of v5, /device:TPU:0, one launch (start us, length us, event | category | flops | bytes accessed | tf_op | source)
XLA Modules:
  0.0 72.6 jit_solution(6297451302348741836)
XLA Ops:
  0.0 0.8 %or_or_fusion = (s32[128]{0:T(128)S(1)}, s32[128]{0:T(128)S(1)}, s32[128]{0:T(128)S(1)}, s32[128]{0:T(128)S(1)}) fusion(s32[2048]{0:T(1024)} %param.23, s32[]{:T(128)S(6)} %select_n.35, s32[2048]{0:T(1024)} %param.22, s32[2048]{0:T(1024)} %param.20, s32[2048,1]{0,1:T(1,128)} %param.21, s32[2048,1]{0,1:T(1,128)} %param.19), kind=kLoop, calls=%fused_computation.15 | loop fusion | flops 1920 | bytes 4612 | tf_op jit(solution)/shard_map/or | solution.py:437
  0.8 0.2 convert_reduce_fusion.1
  1.0 0.2 convert_reduce_fusion
  1.2 0.2 select_reduce_fusion
  1.4 0.0 copy-start
  1.4 0.0 copy-start.1
  1.4 0.1 lt.90
  1.5 0.1 and.56
  1.6 0.1 and.61
  1.6 0.1 and.59
  1.7 0.1 and.64
  1.8 0.1 broadcast_in_dim.66
  1.9 0.1 broadcast_in_dim.67
  2.1 0.1 broadcast_in_dim.63
  2.2 0.1 broadcast_in_dim.64
  2.3 0.1 lt.95
  2.4 0.1 lt.96
  2.5 0.1 lt.92
  2.6 0.1 lt.93
  2.7 0.7 compare_select_fusion
  3.5 0.0 copy-done
  3.5 0.0 copy-done.1
  3.5 67.4 %hessian_kernel.1 = f32[8,8192]{1,0:T(8,128)} custom-call(f32[4]{0:T(128)} %contrast.1, s32[256]{0:T(256)} %copy-done.1, s32[256]{0:T(256)} %copy-done, s32[32,1,256]{2,1,0:T(1,128)} %get-tuple-element.12.row_lanes, s32[32,1,256]{2,1,0:T(1,128)} %get-tuple-element.11.col_lanes, f32[8,8192]{1,0:T(8,128)} %probes.1, f32[1,8192]{1,0:T(1,128)} %bitcast.10, ...), custom_call_target="tpu_custom_call" | custom-call | tf_op jit(solution)/shard_map/hessian_kernel/pallas_call | solution.py:462
  70.9 1.7 %copy.14 = f32[8,8192]{1,0:T(8,128)} copy(f32[8,8192]{1,0:T(8,128)} %hessian_kernel.1) | data formatting | bytes 524288
  (5 shorter events, 0.0 us)
Async XLA Ops:
  1.4 2.1 %copy-start = (s32[256]{0:T(256)}, s32[256]{0:T(256)S(1)}, u32[]{:S(2)}) copy-start(s32[256]{0:T(256)S(1)} %get-tuple-element.17.col_codes) | copy-start | bytes 3076
  1.4 2.1 %copy-start.1 = (s32[256]{0:T(256)}, s32[256]{0:T(256)S(1)}, u32[]{:S(2)}) copy-start(s32[256]{0:T(256)S(1)} %get-tuple-element.18.row_codes) | copy-start | bytes 3076

commit v6 on v4

--- a/solution.py
+++ b/solution.py
@@ -37,7 +37,7 @@
     )
 
 
-def gather_shards(lines, parts, fill, own, out, local_sem, sems, step, side, core):
+def gather_shards(lines, parts, own, out, local_sem, sems, step, side, core):
     send_z, recv_z, send_y, recv_y, send_c, recv_c = sems
     me = index_of(step, side, core)
     across = index_of(step, 1 - side, core)
@@ -58,7 +58,6 @@
         remote(at(slot, p), at(slot, p), recv, recv, peer).wait_recv()
 
     for p in range(parts):
-        fill(p)
         piece = own.at[pl.ds(p * size, size)]
         go(piece, me, p, send_y.at[0, p], recv_y.at[0, p], across)
         for d in range(1, lines):
@@ -282,9 +281,11 @@
             scaling = cell_scaling(level[:, cut], label[:, cut], contrast, units)
             own_cells[b] = halves(probes[:, cut] * scaling).astype(BF16)
 
+    for p in range(parts):
+        fill(p)
     pl.semaphore_wait(barrier, pairs)
     pending = gather_shards(
-        lines, parts, fill, own_cells, cells, cells_sem, gather, step, side, core
+        lines, parts, own_cells, cells, cells_sem, gather, step, side, core
     )
     u_copy.wait()
     v_copy.wait()

time: 72.4 us -> 72.4 us (level)
  no operation moved by 1% of the time
where the time goes in v6:
time: 72.4 us; the launch traced here: 72.2 us
  Pallas kernels  67.1 us (93%)
  local copies, waits for them, and re-layouts  2.95 us (4%)
  other arithmetic  2.04 us (3%)
    pallas_call x1, Pallas kernels, shards(): pl.pallas_call(functools.partial(whole_kernel, lines, units, parts, capac...  67.1 us
    unnamed x5, local copies, waits for them, and re-layouts  1.68 us

profile of v6, /device:TPU:0, one launch (start us, length us, event | category | flops | bytes accessed | tf_op | source)
XLA Modules:
  0.0 72.2 jit_solution(4849416524851632467)
XLA Ops:
  0.0 0.8 %or_or_fusion = (s32[128]{0:T(128)S(1)}, s32[128]{0:T(128)S(1)}, s32[128]{0:T(128)S(1)}, s32[128]{0:T(128)S(1)}) fusion(s32[2048]{0:T(1024)} %param.23, s32[]{:T(128)S(6)} %select_n.35, s32[2048]{0:T(1024)} %param.22, s32[2048]{0:T(1024)} %param.20, s32[2048,1]{0,1:T(1,128)} %param.21, s32[2048,1]{0,1:T(1,128)} %param.19), kind=kLoop, calls=%fused_computation.15 | loop fusion | flops 1920 | bytes 4612 | tf_op jit(solution)/shard_map/or | solution.py:429
  0.8 0.2 convert_reduce_fusion.1
  1.0 0.2 convert_reduce_fusion
  1.2 0.2 select_reduce_fusion
  1.4 0.0 copy-start
  1.4 0.0 copy-start.1
  1.4 0.1 lt.90
  1.5 0.1 and.56
  1.6 0.1 and.61
  1.6 0.1 and.59
  1.7 0.1 and.64
  1.8 0.1 broadcast_in_dim.66
  1.9 0.1 broadcast_in_dim.67
  2.1 0.1 broadcast_in_dim.63
  2.2 0.1 broadcast_in_dim.64
  2.3 0.1 lt.95
  2.4 0.1 lt.96
  2.5 0.1 lt.92
  2.6 0.1 lt.93
  2.7 0.7 compare_select_fusion
  3.5 0.0 copy-done
  3.5 0.0 copy-done.1
  3.5 67.1 %hessian_kernel.1 = f32[8,8192]{1,0:T(8,128)} custom-call(f32[4]{0:T(128)} %contrast.1, s32[256]{0:T(256)} %copy-done.1, s32[256]{0:T(256)} %copy-done, s32[32,1,256]{2,1,0:T(1,128)} %get-tuple-element.12.row_lanes, s32[32,1,256]{2,1,0:T(1,128)} %get-tuple-element.11.col_lanes, f32[8,8192]{1,0:T(8,128)} %probes.1, f32[1,8192]{1,0:T(1,128)} %bitcast.10, ...), custom_call_target="tpu_custom_call" | custom-call | tf_op jit(solution)/shard_map/hessian_kernel/pallas_call | solution.py:454
  70.5 1.7 %copy.14 = f32[8,8192]{1,0:T(8,128)} copy(f32[8,8192]{1,0:T(8,128)} %hessian_kernel.1) | data formatting | bytes 524288
  (5 shorter events, 0.0 us)
Async XLA Ops:
  1.4 2.1 %copy-start = (s32[256]{0:T(256)}, s32[256]{0:T(256)S(1)}, u32[]{:S(2)}) copy-start(s32[256]{0:T(256)S(1)} %get-tuple-element.17.col_codes) | copy-start | bytes 3076
  1.4 2.1 %copy-start.1 = (s32[256]{0:T(256)}, s32[256]{0:T(256)S(1)}, u32[]{:S(2)}) copy-start(s32[256]{0:T(256)S(1)} %get-tuple-element.18.row_codes) | copy-start | bytes 3076
